TPU v7x, 32 devices: a whole 2x2x4 slice. The times are simulated.
32 devices in a mesh: noise: 2 (over x), row: 4 (over y, core), col: 4 (over z).
Axes of the slice: x: 2, y: 2, z: 4, core: 2. Of those that a mesh axis runs over, the one named last changes fastest.
Arguments:
- image: bfloat16 [256, 128, 128], P(('noise', 'row'), 'col'), parts along dimension 0, may hold values from -6 to 6
- noise_level: int32 [2], P('noise'), parts along dimension 0, may hold values from 0 to 7
- cond_table: float32 [8, 256], replicated, may hold values from -6 to 6
- ada_fine: float32 [256, 128], replicated, may hold values from -0.375 to 0.375
- fine_qkv: bfloat16 [128, 384], replicated, may hold values from -0.5 to 0.5
- fine_scale: float32 [2], replicated, may hold values from 4 to 16
- fine_out_w: bfloat16 [128, 128], replicated, may hold values from -0.5 to 0.5
- fine_post: float32 [128], replicated, may hold values from 0.1 to 1.9
- merge_w: bfloat16 [512, 256], replicated, may hold values from -0.25 to 0.25
- coarse_in_w: bfloat16 [256, 1024], replicated, may hold values from -0.375 to 0.375
- ada_coarse: float32 [256, 1024], replicated, may hold values from -0.375 to 0.375
- coarse_qkv: bfloat16 [3, 1024, 1024], P(None, None, 'col'), may hold values from -0.1875 to 0.1875
- coarse_scale: float32 [16], P('col'), may hold values from 4 to 16
- coarse_out_w: bfloat16 [1024, 1024], P('col'), may hold values from -0.1875 to 0.1875
- coarse_post: float32 [1024], replicated, may hold values from 0.1 to 1.9
Outputs:
- fine_out: bfloat16 [256, 128, 128], P(('noise', 'row'), 'col'), parts along dimension 0
- coarse_out: bfloat16 [16, 8, 1024], P(('noise', 'row'), 'col'), parts along dimension 0
There are 2 independent parts, one for each index of `noise`. A program takes and returns all parts, laid end to end along the dimension named above; an argument that names none is the same for every part. Nothing has to cross between parts.
All inputs are finite; a program needn't handle non-finite values.
Results may differ from a plain program's by a relative error of at most 0.035.
Values may be sent and summed in bfloat16 or wider, within the bound.
A program may use at most 128 MiB of HBM per device.

v0:
```python
import jax
import jax.numpy as jnp
from jax import lax
from jax.sharding import PartitionSpec as P

HEAD = 64
TILE = 32
POOL = 8


def with_halo(x, sides, width):
    for axis, dim in sides:
        devices, length = (lax.axis_size(axis), x.shape[dim])
        up = [(i, (i + 1) % devices) for i in range(devices - 1)]
        down = [(j, i) for i, j in up]
        last = lax.slice_in_dim(x, length - width, length, axis=dim)
        initial = lax.slice_in_dim(x, 0, width, axis=dim)
        before = lax.ppermute(last, axis, up)
        after = lax.ppermute(initial, axis, down)
        x = jnp.concatenate([before, x, after], axis=dim)
    return x


def rms(value):
    return value * lax.rsqrt(jnp.mean(value * value, axis=-1, keepdims=True) + 1e-06)


def cosine(value, heads):
    shaped = value.reshape(value.shape[:-1] + (heads, HEAD))
    return rms(shaped).reshape(value.shape)


def attend(queries, keys, values, valid, scale, heads):
    results = []
    for head in range(heads):
        low = head * HEAD
        scores = jnp.dot(
            queries[:, low : low + HEAD],
            keys[:, low : low + HEAD].T,
            preferred_element_type=jnp.float32,
        )
        scores = scores * (scale[head] / HEAD)
        if valid is not None:
            scores = jnp.where(valid[None, :], scores, -jnp.inf)
        top = jnp.max(scores, axis=-1, keepdims=True)
        expo = jnp.exp(scores - top)
        if valid is not None:
            expo = jnp.where(valid[None, :], expo, 0.0)
        weights = (expo / jnp.sum(expo, axis=-1, keepdims=True)).astype(jnp.bfloat16)
        results.append(
            jnp.dot(weights, values[:, low : low + HEAD], preferred_element_type=jnp.float32)
        )
    return jnp.concatenate(results, axis=-1).astype(jnp.bfloat16)


def attend_blocks(queries, keys, values, valid, scale, heads):
    count, width = queries.shape
    block = min(512, count)
    grouped = queries.reshape(count // block, block, width)

    def one_block(part_q):
        return attend(part_q, keys, values, valid, scale, heads)

    return lax.map(one_block, grouped).reshape(count, width)


def body(
    image,
    noise_level,
    cond_table,
    ada_fine,
    fine_qkv,
    fine_scale,
    fine_out_w,
    fine_post,
    merge_w,
    coarse_in_w,
    ada_coarse,
    coarse_qkv,
    coarse_scale,
    coarse_out_w,
    coarse_post,
):
    highest = lax.Precision.HIGHEST
    tile = TILE
    rows_loc, cols_loc, width = image.shape
    heads = width // HEAD
    levels = jnp.arange(cond_table.shape[0], dtype=jnp.int32)
    hot = (levels == noise_level[0]).astype(jnp.float32)
    cond = jnp.dot(hot, cond_table, precision=highest)
    fine_gain = 1.0 + jnp.dot(cond, ada_fine, precision=highest)
    coarse_gain = 1.0 + jnp.dot(cond, ada_coarse, precision=highest)
    xfull = image.astype(jnp.float32)
    xn = (rms(xfull) * fine_gain).astype(jnp.bfloat16)
    qproj = jnp.dot(xn.reshape(-1, width), fine_qkv[:, :width], preferred_element_type=jnp.float32)
    queries = cosine(qproj, heads).astype(jnp.bfloat16).reshape(rows_loc, cols_loc, width)
    shape = xn.shape[:2]
    proj = jnp.dot(xn.reshape(-1, width), fine_qkv[:, width:], preferred_element_type=jnp.float32)
    proj = proj.reshape(shape + (2 * width,))
    keys_out = cosine(proj[..., :width], heads).astype(jnp.bfloat16)
    values_out = proj[..., width:].astype(jnp.bfloat16)
    both = jnp.stack([keys_out, values_out], axis=0)
    padded = with_halo(both, (("row", 1), ("col", 2)), tile)
    keys_pad = padded[0]
    values_pad = padded[1]
    grid_rows = rows_loc * lax.axis_size("row")
    grid_cols = cols_loc * lax.axis_size("col")
    row_ids = (
        lax.axis_index("row") * rows_loc - tile + jnp.arange(rows_loc + 2 * tile, dtype=jnp.int32)
    )
    col_ids = (
        lax.axis_index("col") * cols_loc - tile + jnp.arange(cols_loc + 2 * tile, dtype=jnp.int32)
    )
    row_ok = (row_ids >= 0) & (row_ids < grid_rows)
    col_ok = (col_ids >= 0) & (col_ids < grid_cols)
    q_tile = queries.reshape(tile * tile, width)
    k_win = keys_pad.reshape(-1, width)
    v_win = values_pad.reshape(-1, width)
    valid = (row_ok[:, None] & col_ok[None, 0 : 3 * tile]).reshape(-1)
    result = attend_blocks(q_tile, k_win, v_win, valid, fine_scale, heads)
    pieces = [result.reshape(tile, tile, width)]
    attended = jnp.concatenate(pieces, axis=1)
    branch = jnp.dot(attended.reshape(-1, width), fine_out_w, preferred_element_type=jnp.float32)
    branch = branch.reshape(rows_loc, cols_loc, width)
    fine_out = (xfull + rms(branch) * fine_post).astype(jnp.bfloat16)
    merge_width = merge_w.shape[1]
    blocks = (
        fine_out.reshape(rows_loc // 2, 2, cols_loc // 2, 2, width)
        .transpose(0, 2, 1, 3, 4)
        .reshape(-1, 4 * width)
    )
    merged = jnp.dot(blocks, merge_w, preferred_element_type=jnp.float32).astype(jnp.bfloat16)
    pool_rows = rows_loc // (2 * POOL)
    pool_cols = cols_loc // (2 * POOL)
    merged = merged.reshape(pool_rows, POOL, pool_cols, POOL, merge_width).astype(jnp.float32)
    pooled = jnp.mean(merged, axis=(1, 3)).astype(jnp.bfloat16).reshape(-1, merge_width)
    coarse_in = jnp.dot(pooled, coarse_in_w, preferred_element_type=jnp.float32)
    cn = (rms(coarse_in) * coarse_gain).astype(jnp.bfloat16)
    coarse_width = cn.shape[1]
    local_width = coarse_qkv.shape[2]
    local_heads = local_width // HEAD
    proj = jnp.einsum(
        "nd,kde->kne",
        lax.all_gather(cn, ("row", "col"), axis=0, tiled=True),
        coarse_qkv,
        preferred_element_type=jnp.float32,
    )
    q_part = cosine(proj[0], local_heads)
    k_part = cosine(proj[1], local_heads)
    projected = jnp.concatenate([q_part, k_part, proj[2]], axis=-1).astype(jnp.bfloat16)
    own_count = cn.shape[0]
    row_count = own_count * lax.axis_size("col")
    row_start = lax.axis_index("row") * row_count
    q_rows = lax.dynamic_slice_in_dim(projected[:, :local_width], row_start, row_count, 0)
    k_all = projected[:, local_width : 2 * local_width]
    v_all = projected[:, 2 * local_width :]
    coarse_attended = attend(q_rows, k_all, v_all, None, coarse_scale, local_heads)
    coarse_branch = lax.psum_scatter(
        jnp.dot(coarse_attended, coarse_out_w, preferred_element_type=jnp.float32).astype(
            jnp.bfloat16
        ),
        "col",
        scatter_dimension=0,
        tiled=True,
    ).astype(jnp.float32)
    coarse_out = (coarse_in + rms(coarse_branch) * coarse_post).astype(jnp.bfloat16)
    coarse_out = coarse_out.reshape(pool_rows, pool_cols, coarse_width)
    return (fine_out, coarse_out)


def solution(mesh):
    in_specs = (
        P(("noise", "row"), "col", None),
        P("noise"),
        P(),
        P(),
        P(),
        P(),
        P(),
        P(),
        P(),
        P(),
        P(),
        P(None, None, "col"),
        P("col"),
        P("col", None),
        P(),
    )
    out_specs = (P(("noise", "row"), "col", None), P(("noise", "row"), "col", None))
    return jax.shard_map(body, mesh=mesh, in_specs=in_specs, out_specs=out_specs, check_vma=False)
```

profile of v0, /device:TPU:0, one launch (start us, length us, event | category | flops | bytes accessed | tf_op | source)
XLA Modules:
  0.0 261.7 jit_solution(5432970516299385419)
XLA Ops:
  1.4 1.2 fusion.33
  2.6 0.8 convolution_bitcast_fusion.1
  3.4 1.1 fusion.32
  4.5 1.2 fusion.35
  5.7 1.1 fusion.40
  6.8 0.9 slice_multiply_fusion
  7.7 2.6 %mul.210 = f32[32,32,2,64]{3,2,1,0:T(2,128)} reshape(f32[32,32,128]{2,1,0:T(8,128)} %slice_multiply_fusion) | data formatting | bytes 1048576 | tf_op jit(solution)/shard_map/mul | solution.py:25
  10.4 3.2 %reduce_sum.141 = f32[32,32,2]{2,1,0:T(8,128)} reduce(f32[32,32,2,64]{3,2,1,0:T(2,128)} %mul.210, f32[]{:T(128)} %constant.82.clone.1), dimensions={3}, to_apply=%region_2.0 | reduce | flops 129024 | bytes 532484 | tf_op jit(solution)/shard_map/reduce_sum | solution.py:25
  13.6 1.3 copy.35
  15.0 1.1 copy.36
  16.0 3.0 %mul.211 = f32[32,32,2,64]{3,2,1,0:T(2,128)} broadcast(f32[32,32,2]{2,1,0:T(8,128)} %copy.36), dimensions={0,1,2} | broadcast | bytes 532480 | tf_op jit(solution)/shard_map/mul | solution.py:25
  19.0 2.6 %mul.212 = f32[32,32,128]{2,1,0:T(8,128)} reshape(f32[32,32,2,64]{3,2,1,0:T(2,128)} %mul.211) | data formatting | bytes 1048576 | tf_op jit(solution)/shard_map/mul | solution.py:25
  21.7 1.1 fusion.37
  22.9 2.4 collective-permute-start
  25.3 1.3 collective-permute-start.1
  26.7 4.4 %collective-permute-done.1 = bf16[2,32,32,128]{3,2,1,0:T(8,128)(2,1)S(1)} collective-permute-done((bf16[2,32,32,128]{3,2,1,0:T(8,128)(2,1)S(1)}, bf16[2,32,32,128]{3,2,1,0:T(8,128)(2,1)S(1)}, u32[]{:S(2)}, u32[]{:S(2)}) %collective-permute-start.1) | collective-permute-done | bytes 524320 | tf_op jit(solution)/shard_map/ppermute | solution.py:19
  31.2 0.8 copy-done.4
  32.0 1.3 pad_maximum_fusion.2
  33.3 4.6 %collective-permute-start.2 = (bf16[2,96,32,128]{3,2,1,0:T(8,128)(2,1)}, bf16[2,96,32,128]{3,2,1,0:T(8,128)(2,1)}, u32[]{:S(2)}, u32[]{:S(2)}) collective-permute-start(bf16[2,96,32,128]{3,2,1,0:T(8,128)(2,1)} %pad_maximum_fusion.2), channel_id=1, source_target_pairs={{0,1},{1,2},{2,3},{4,5},{5,6},{6,7},{8,9},{9,10},{10,11},{12,13},{... | collective-permute-start | bytes 4718600 | tf_op jit(solution)/shard_map/ppermute | solution.py:18
  37.9 1.3 collective-permute-start.3
  39.2 0.8 slice_bitcast_fusion.1
  40.8 0.6 fusion.90
  42.7 0.7 fusion.89
  45.9 0.6 dynamic-slice
  47.2 1.8 fusion.95
  49.0 0.6 broadcast_add_fusion
  49.6 15.9 %collective-permute-done.2 = bf16[2,96,32,128]{3,2,1,0:T(8,128)(2,1)} collective-permute-done((bf16[2,96,32,128]{3,2,1,0:T(8,128)(2,1)}, bf16[2,96,32,128]{3,2,1,0:T(8,128)(2,1)}, u32[]{:S(2)}, u32[]{:S(2)}) %collective-permute-start.2) | collective-permute-done | bytes 1572896 | tf_op jit(solution)/shard_map/ppermute | solution.py:18
  65.6 5.8 %collective-permute-done.3 = bf16[2,96,32,128]{3,2,1,0:T(8,128)(2,1)} collective-permute-done((bf16[2,96,32,128]{3,2,1,0:T(8,128)(2,1)}, bf16[2,96,32,128]{3,2,1,0:T(8,128)(2,1)}, u32[]{:S(2)}, u32[]{:S(2)}) %collective-permute-start.3) | collective-permute-done | bytes 1572896 | tf_op jit(solution)/shard_map/ppermute | solution.py:19
  71.4 7.0 %pad_maximum_fusion.1 = bf16[2,96,96,128]{3,2,1,0:T(8,128)(2,1)S(1)} fusion(bf16[2,96,32,128]{3,2,1,0:T(8,128)(2,1)} %collective-permute-done.3, bf16[2,32,32,128]{3,2,1,0:T(8,128)(2,1)} %copy-done.4, bf16[1,32,32,128]{3,2,1,0:T(8,128)(2,1)S(1)} %fusion.38, bf16[1,32,32,128]{3,2,1,0:T(8,128)(2,1)S(1)} %fusion.37, ...), kind=kLoop, calls=%fused_computation.33 | loop fusion | flops 28311552 | bytes 9437184 | tf_op jit(solution)/shard_map/concatenate | solution.py:20
  78.4 3.0 %fusion.88 = (bf16[1,96,96,128]{3,2,1,0:T(8,128)(2,1)}, bf16[1,96,96,128]{3,2,1,0:T(8,128)(2,1)}) fusion(bf16[2,96,96,128]{3,2,1,0:T(8,128)(2,1)S(1)} %pad_maximum_fusion.1), kind=kLoop, calls=%fused_computation.147 | loop fusion | bytes 9437184 | tf_op jit(solution)/shard_map/slice | solution.py:105
  81.4 121.4 %while.13 = (s32[]{:T(128)}, bf16[2,512,128]{2,1,0:T(8,128)(2,1)S(1)}, bf16[2,512,128]{2,1,0:T(8,128)(2,1)S(1)}, bf16[9216,128]{1,0:T(8,128)(2,1)}, f32[]{:T(128...) while((s32[]{:T(128)}, ...), condition=%wide.region_8.9_spmd.clone, body=%wide.region_3.8_spmd.clone.sunk | while | flops 2548374528 | bytes 143094144 | solution.py:64
  81.8 9.7 %fusion.121 = (f32[512]{0:T(512)S(1)}, f32[512,9216]{1,0:T(8,128)}) fusion(f32[]{:T(128)} %get-tuple-element.297, pred[9216]{0:T(1024)(128)(4,1)S(1)} %broadcast_in_dim.147, bf16[9216,128]{1,0:T(8,128)(2,1)} %get-tuple-element.296, bf16[512,128]{1,0:T(8,128)(2,1)S(1)} %dynamic-slice_bitcast_fusion.2), kind=kOutput, calls=%fused_computation.7.clone.1 | convolution fusion | flops 618135040 | bytes 21376004 | tf_op jit(solution)/shard_map/while/body/eval_jaxpr/dot_general | solution.py:37
  91.5 18.1 %fusion.122 = (f32[512]{0:T(512)S(1)}, f32[512]{0:T(512)S(1)}, f32[512,9216]{1,0:T(8,128)}) fusion(f32[512,9216]{1,0:T(8,128)} %get-tuple-element.268, f32[512]{0:T(512)S(1)} %get-tuple-element.269, f32[]{:T(128)} %get-tuple-element.297, pred[9216]{0:T(1024)(128)(4,1)S(1)} %broadcast_in_dim.147, f32[]{:T(128)} %get-tuple-element.299, ...), kind=kOutput, calls=%fused_computation.9.clone.1 | convolution fusion | flops 641727488 | bytes 40254472 | tf_op jit(solution)/shard_map/while/body/eval_jaxpr/dot_general | solution.py:37
  109.7 9.4 %fusion.125 = bf16[1,512,64]{1,2,0:T(8,128)(2,1)S(1)} fusion(bf16[9216,128]{1,0:T(8,128)(2,1)S(1)} %copy-done.3, f32[512,9216]{1,0:T(8,128)} %get-tuple-element.268, f32[512]{0:T(512)S(1)} %get-tuple-element.272, f32[512]{0:T(512)S(1)} %get-tuple-element.269, f32[]{:T(128)} %get-tuple-element.297, pred[9216]{0:T(1024)(128)(4,1)S(1)} %broadcast_in_dim.147), kind=kOutput, calls=%fused_computation.21.clone.1 | convolution fusion | flops 632324096 | bytes 21312516 | tf_op jit(solution)/shard_map/while/body/eval_jaxpr/dot_general | solution.py:51
  119.1 11.7 %fusion.123 = f32[512]{0:T(512)S(1)} fusion(f32[512,9216]{1,0:T(8,128)} %get-tuple-element.270, f32[512]{0:T(512)S(1)} %get-tuple-element.271, f32[]{:T(128)} %get-tuple-element.299, pred[9216]{0:T(1024)(128)(4,1)S(1)} %broadcast_in_dim.147), kind=kLoop, calls=%fused_computation.10.clone.1 | loop fusion | flops 23592448 | bytes 18887684 | tf_op jit(solution)/shard_map/while/body/eval_jaxpr/reduce_sum | solution.py:49
  130.8 11.1 %fusion.124 = bf16[1,512,64]{1,2,0:T(8,128)(2,1)S(1)} fusion(bf16[9216,128]{1,0:T(8,128)(2,1)} %get-tuple-element.298, f32[512,9216]{1,0:T(8,128)} %get-tuple-element.270, f32[512]{0:T(512)S(1)} %fusion.123, f32[512]{0:T(512)S(1)} %get-tuple-element.271, f32[]{:T(128)} %get-tuple-element.299, pred[9216]{0:T(1024)(128)(4,1)S(1)} %broadcast_in_dim.147), kind=kOutput, calls=%fused_computation.22.clone.1 | convolution fusion | flops 632324096 | bytes 21312516 | tf_op jit(solution)/shard_map/while/body/eval_jaxpr/dot_general | solution.py:51
  142.3 9.7 %fusion.121 = (f32[512]{0:T(512)S(1)}, f32[512,9216]{1,0:T(8,128)}) fusion(f32[]{:T(128)} %get-tuple-element.297, pred[9216]{0:T(1024)(128)(4,1)S(1)} %broadcast_in_dim.147, bf16[9216,128]{1,0:T(8,128)(2,1)} %get-tuple-element.296, bf16[512,128]{1,0:T(8,128)(2,1)S(1)} %dynamic-slice_bitcast_fusion.2), kind=kOutput, calls=%fused_computation.7.clone.1 | convolution fusion | flops 618135040 | bytes 21376004 | tf_op jit(solution)/shard_map/while/body/eval_jaxpr/dot_general | solution.py:37
  152.0 18.1 %fusion.122 = (f32[512]{0:T(512)S(1)}, f32[512]{0:T(512)S(1)}, f32[512,9216]{1,0:T(8,128)}) fusion(f32[512,9216]{1,0:T(8,128)} %get-tuple-element.268, f32[512]{0:T(512)S(1)} %get-tuple-element.269, f32[]{:T(128)} %get-tuple-element.297, pred[9216]{0:T(1024)(128)(4,1)S(1)} %broadcast_in_dim.147, f32[]{:T(128)} %get-tuple-element.299, ...), kind=kOutput, calls=%fused_computation.9.clone.1 | convolution fusion | flops 641727488 | bytes 40254472 | tf_op jit(solution)/shard_map/while/body/eval_jaxpr/dot_general | solution.py:37
  170.1 9.4 %fusion.125 = bf16[1,512,64]{1,2,0:T(8,128)(2,1)S(1)} fusion(bf16[9216,128]{1,0:T(8,128)(2,1)S(1)} %copy-done.3, f32[512,9216]{1,0:T(8,128)} %get-tuple-element.268, f32[512]{0:T(512)S(1)} %get-tuple-element.272, f32[512]{0:T(512)S(1)} %get-tuple-element.269, f32[]{:T(128)} %get-tuple-element.297, pred[9216]{0:T(1024)(128)(4,1)S(1)} %broadcast_in_dim.147), kind=kOutput, calls=%fused_computation.21.clone.1 | convolution fusion | flops 632324096 | bytes 21312516 | tf_op jit(solution)/shard_map/while/body/eval_jaxpr/dot_general | solution.py:51
  179.6 11.7 %fusion.123 = f32[512]{0:T(512)S(1)} fusion(f32[512,9216]{1,0:T(8,128)} %get-tuple-element.270, f32[512]{0:T(512)S(1)} %get-tuple-element.271, f32[]{:T(128)} %get-tuple-element.299, pred[9216]{0:T(1024)(128)(4,1)S(1)} %broadcast_in_dim.147), kind=kLoop, calls=%fused_computation.10.clone.1 | loop fusion | flops 23592448 | bytes 18887684 | tf_op jit(solution)/shard_map/while/body/eval_jaxpr/reduce_sum | solution.py:49
  191.3 11.1 %fusion.124 = bf16[1,512,64]{1,2,0:T(8,128)(2,1)S(1)} fusion(bf16[9216,128]{1,0:T(8,128)(2,1)} %get-tuple-element.298, f32[512,9216]{1,0:T(8,128)} %get-tuple-element.270, f32[512]{0:T(512)S(1)} %fusion.123, f32[512]{0:T(512)S(1)} %get-tuple-element.271, f32[]{:T(128)} %get-tuple-element.299, pred[9216]{0:T(1024)(128)(4,1)S(1)} %broadcast_in_dim.147), kind=kOutput, calls=%fused_computation.22.clone.1 | convolution fusion | flops 632324096 | bytes 21312516 | tf_op jit(solution)/shard_map/while/body/eval_jaxpr/dot_general | solution.py:51
  202.8 0.4 multiply_reduce_fusion
  203.7 1.2 convolution_convert_fusion
  205.4 32.3 %all-gather = bf16[16,4,1024]{2,1,0:T(4,128)(2,1)S(1)} all-gather(bf16[1,4,1024]{2,1,0:T(4,128)(2,1)S(1)} %fusion.59), channel_id=1, replica_groups=mesh['noise'=2,'row'=4,'col'=4] {'row','col'}, dimensions={0}, use_global_device_ids=true | all-gather | bytes 139264 | tf_op jit(solution)/shard_map/all_gather | solution.py:144
  237.7 0.4 convolution_bitcast_fusion
  242.0 1.3 convolution_convert_fusion.1
  243.2 17.6 %all-reduce = bf16[16,1024]{1,0:T(8,128)(2,1)S(1)} all-reduce(bf16[16,1024]{1,0:T(8,128)(2,1)S(1)} %convolution_convert_fusion.1), channel_id=2, replica_groups=mesh['noise'=2,'row'=4,'col'=4] {'col'}, use_global_device_ids=true, to_apply=%region_22.23.clone | all-reduce | flops 16384 | bytes 65536
  261.1 0.6 reshape.193
  (98 shorter events, 6.9 us)
Async XLA Ops:
  0.6 237.0 %copy-start = (bf16[3,1024,256]{2,1,0:T(8,128)(2,1)S(1)}, bf16[3,1024,256]{2,1,0:T(8,128)(2,1)}, u32[]{:S(2)}) copy-start(bf16[3,1024,256]{2,1,0:T(8,128)(2,1)} %param.28) | copy-start | bytes 4718596
  5.7 35.2 %copy-start.12 = (f32[2]{0:T(128)S(1)}, f32[2]{0:T(128)}, u32[]{:S(2)}) copy-start(f32[2]{0:T(128)} %param.22) | copy-start | bytes 28
  5.7 37.0 %copy-start.10 = (f32[4]{0:T(128)S(1)}, f32[4]{0:T(128)}, u32[]{:S(2)}) copy-start(f32[4]{0:T(128)} %param.29) | copy-start | bytes 52
  5.7 40.2 %copy-start.14 = (u32[32]{0:T(128)S(1)}, u32[32]{0:T(128)}, u32[]{:S(2)}) copy-start(u32[32]{0:T(128)} %constant.100) | copy-start | bytes 388
  22.9 3.9 %collective-permute-start = (bf16[2,32,32,128]{3,2,1,0:T(8,128)(2,1)S(1)}, bf16[2,32,32,128]{3,2,1,0:T(8,128)(2,1)S(1)}, u32[]{:S(2)}, u32[]{:S(2)}) collective-permute-start(bf16[2,32,32,128]{3,2,1,0:T(8,128)(2,1)S(1)} %pad_maximum_fusion.3), channel_id=1, source_target_pairs={{0,4},{4,8},{8,12},{1,5},{5,9},{9,13},{2,6},{6,10},{10,14},{3,7},{... | collective-permute-start | bytes 1572872 | tf_op jit(solution)/shard_map/ppermute | solution.py:18
  25.3 5.9 %collective-permute-start.1 = (bf16[2,32,32,128]{3,2,1,0:T(8,128)(2,1)S(1)}, bf16[2,32,32,128]{3,2,1,0:T(8,128)(2,1)S(1)}, u32[]{:S(2)}, u32[]{:S(2)}) collective-permute-start(bf16[2,32,32,128]{3,2,1,0:T(8,128)(2,1)S(1)} %pad_maximum_fusion.3), channel_id=1, source_target_pairs={{4,0},{8,4},{12,8},{5,1},{9,5},{13,9},{6,2},{10,6},{14,10},{7,3},{... | collective-permute-start | bytes 1572872 | tf_op jit(solution)/shard_map/ppermute | solution.py:19
  31.2 0.8 copy-start.4
  33.3 32.3 %collective-permute-start.2 = (bf16[2,96,32,128]{3,2,1,0:T(8,128)(2,1)}, bf16[2,96,32,128]{3,2,1,0:T(8,128)(2,1)}, u32[]{:S(2)}, u32[]{:S(2)}) collective-permute-start(bf16[2,96,32,128]{3,2,1,0:T(8,128)(2,1)} %pad_maximum_fusion.2), channel_id=1, source_target_pairs={{0,1},{1,2},{2,3},{4,5},{5,6},{6,7},{8,9},{9,10},{10,11},{12,13},{... | collective-permute-start | bytes 4718600 | tf_op jit(solution)/shard_map/ppermute | solution.py:18
  37.9 33.5 %collective-permute-start.3 = (bf16[2,96,32,128]{3,2,1,0:T(8,128)(2,1)}, bf16[2,96,32,128]{3,2,1,0:T(8,128)(2,1)}, u32[]{:S(2)}, u32[]{:S(2)}) collective-permute-start(bf16[2,96,32,128]{3,2,1,0:T(8,128)(2,1)} %pad_maximum_fusion.2), channel_id=1, source_target_pairs={{1,0},{2,1},{3,2},{5,4},{6,5},{7,6},{9,8},{10,9},{11,10},{13,12},{... | collective-permute-start | bytes 4718600 | tf_op jit(solution)/shard_map/ppermute | solution.py:19
  49.6 31.7 %copy-start.7 = (bf16[2,512,128]{2,1,0:T(8,128)(2,1)S(1)}, bf16[2,512,128]{2,1,0:T(8,128)(2,1)}, u32[]{:S(2)}) copy-start(bf16[2,512,128]{2,1,0:T(8,128)(2,1)} %custom-call) | copy-start | bytes 786436
  81.3 121.4 %copy-start.8 = (bf16[128,128]{1,0:T(8,128)(2,1)S(1)}, bf16[128,128]{1,0:T(8,128)(2,1)}, u32[]{:S(2)}) copy-start(bf16[128,128]{1,0:T(8,128)(2,1)} %param.23) | copy-start | bytes 98308
  81.3 121.8 %copy-start.2 = (bf16[32,32,128]{2,1,0:T(8,128)(2,1)S(1)}, bf16[32,32,128]{2,1,0:T(8,128)(2,1)}, u32[]{:S(2)}) copy-start(bf16[32,32,128]{2,1,0:T(8,128)(2,1)} %param.17) | copy-start | bytes 786436
  81.3 121.8 %copy-start.13 = (f32[128]{0:T(128)S(1)}, f32[128]{0:T(128)}, u32[]{:S(2)}) copy-start(f32[128]{0:T(128)} %param.24) | copy-start | bytes 1540
  81.3 123.6 %copy-start.6 = (bf16[256,1024]{1,0:T(8,128)(2,1)S(1)}, bf16[256,1024]{1,0:T(8,128)(2,1)}, u32[]{:S(2)}) copy-start(bf16[256,1024]{1,0:T(8,128)(2,1)} %param.26) | copy-start | bytes 1572868
  81.4 123.9 %copy-start.9 = (f32[1024]{0:T(1024)S(1)}, f32[1024]{0:T(1024)}, u32[]{:S(2)}) copy-start(f32[1024]{0:T(1024)} %broadcast_add_fusion) | copy-start | bytes 12292
  81.8 9.7 %copy-start.1 = (bf16[9216,128]{1,0:T(8,128)(2,1)S(1)}, bf16[9216,128]{1,0:T(8,128)(2,1)}, u32[]{:S(2)}) copy-start(bf16[9216,128]{1,0:T(8,128)(2,1)} %get-tuple-element.296) | copy-start | bytes 7077892 | tf_op jit(solution)/shard_map/while
  91.5 18.2 %copy-start.3 = (bf16[9216,128]{1,0:T(8,128)(2,1)S(1)}, bf16[9216,128]{1,0:T(8,128)(2,1)}, u32[]{:S(2)}) copy-start(bf16[9216,128]{1,0:T(8,128)(2,1)} %get-tuple-element.298) | copy-start | bytes 7077892 | tf_op jit(solution)/shard_map/while
  142.3 9.7 %copy-start.1 = (bf16[9216,128]{1,0:T(8,128)(2,1)S(1)}, bf16[9216,128]{1,0:T(8,128)(2,1)}, u32[]{:S(2)}) copy-start(bf16[9216,128]{1,0:T(8,128)(2,1)} %get-tuple-element.296) | copy-start | bytes 7077892 | tf_op jit(solution)/shard_map/while
  152.0 18.1 %copy-start.3 = (bf16[9216,128]{1,0:T(8,128)(2,1)S(1)}, bf16[9216,128]{1,0:T(8,128)(2,1)}, u32[]{:S(2)}) copy-start(bf16[9216,128]{1,0:T(8,128)(2,1)} %get-tuple-element.298) | copy-start | bytes 7077892 | tf_op jit(solution)/shard_map/while
  202.8 58.3 %copy-start.11 = (f32[1024]{0:T(1024)S(1)}, f32[1024]{0:T(1024)}, u32[]{:S(2)}) copy-start(f32[1024]{0:T(1024)} %param.31) | copy-start | bytes 12292
  203.4 58.3 %copy-start.5 = (bf16[32,32,128]{2,1,0:T(8,128)(2,1)}, bf16[32,32,128]{2,1,0:T(8,128)(2,1)S(1)}, u32[]{:S(2)}) copy-start(bf16[32,32,128]{2,1,0:T(8,128)(2,1)S(1)} %fusion.36) | copy-start | bytes 786436
where the time goes:
time: 263 us; the launch traced here: 262 us
  matrix products  107 us (41%)
  blocking collectives  49.9 us (19%)
  other arithmetic  41.9 us (16%)
  waiting for transfers between devices  26.4 us (10%)
  local copies, waits for them, and re-layouts  19.9 us (8%)
  starting transfers between devices  9.58 us (4%)
  between operations  6.37 us (2%)
    dot_general x8, matrix products, attend(): jnp.dot(queries[:, low:low + HEAD], keys[:, low:low + HEAD].T, preferred_...  56.8 us
    dot_general x8, matrix products, attend(): jnp.dot(weights, values[:, low:low + HEAD], preferred_element_type=jnp.fl...  41.7 us
    all_gather x1, blocking collectives, body(): lax.all_gather(cn, ('row', 'col'), axis=0, tiled=True)  32.3 us
    reduce_sum x6, other arithmetic, attend(): jnp.sum(expo, axis=-1, keepdims=True)  24.2 us
    unnamed x1, blocking collectives  17.6 us
    ppermute x2, waiting for transfers between devices, with_halo(): before = lax.ppermute(last, axis, up)  16.1 us
    ppermute x2, waiting for transfers between devices, with_halo(): after = lax.ppermute(initial, axis, down)  10.2 us
    concatenate x2, other arithmetic, with_halo(): x = jnp.concatenate([before, x, after], axis=dim)  8.3 us
  transfers between devices with their start and end apart: 4, of which 4 were waited for; matrix products, arithmetic and copies ran while one was open for 2% of the time, Pallas kernels for 0%

commit v1 on v0

v1 whole, which is shorter than its diff:
```python
import functools
import math

import jax
import jax.numpy as jnp
from jax import lax
from jax.experimental import pallas as pl
from jax.experimental.pallas import tpu as pltpu
from jax.sharding import PartitionSpec as P

HEAD = 64
TILE = 32
POOL = 8
QB = 256
EPS = 1e-6
MESH = pl.DeviceIdType.MESH
HIGHEST = lax.Precision.HIGHEST
BF = jnp.bfloat16
F32 = jnp.float32
SWAP = (0, 2, 1)


def mm(a, b):
    return jnp.dot(a, b, preferred_element_type=F32)


def iota(shape, dim):
    return lax.broadcasted_iota(jnp.int32, shape, dim)


def kernel(
    nrow, ncol, level_ref, fscale_ref, cscale_ref, image_ref, table_ref, ada_fine_ref, fqkv_ref,
    fout_ref, fpost_ref, cpost_ref, merge_hbm, cin_hbm, adac_hbm, cqkv_hbm, cout_hbm,
    fine_ref, coarse_ref,
    slots, qs, kt, vext, acc, merge_w, cin_w, adac_w, cqkv_w, cout_w, gath, pack, qall,
    sbuf, rbuf, local_sem, hsend, hrecv, gsend, grecv, rsend, rrecv,
):
    tokens, width = image_ref.shape
    ndev = nrow * ncol
    row, col = lax.axis_index("row"), lax.axis_index("col")
    me = row * ncol + col
    sib = 1 - 2 * lax.rem(row, 2)

    barrier = pltpu.get_barrier_semaphore()

    def greet(i, carry):
        peer = lax.rem(me + i, ndev)
        pl.semaphore_signal(
            barrier, inc=1, device_id={"row": peer // ncol, "col": lax.rem(peer, ncol)},
            device_id_type=MESH,
        )
        return carry

    lax.fori_loop(1, ndev, greet, 0)
    loads = [
        pltpu.make_async_copy(src, dst, local_sem.at[i])
        for i, (src, dst) in enumerate(
            ((merge_hbm, merge_w), (cin_hbm, cin_w), (adac_hbm, adac_w), (cqkv_hbm, cqkv_w),
             (cout_hbm, cout_w))
        )
    ]
    for load in loads:
        load.start()

    levels = table_ref.shape[0]
    hot = iota((levels, 1), 0) == level_ref[0]
    cond = jnp.sum(jnp.where(hot, table_ref[...], 0.0), axis=0, keepdims=True)
    cond = jnp.broadcast_to(cond, (8, cond.shape[1]))
    fine_gain = 1.0 + jnp.dot(cond, ada_fine_ref[...], precision=HIGHEST)[0:1]
    low = iota((1, width), 1) < HEAD
    same = (iota((width, width), 0) // HEAD) == (iota((width, width), 1) // HEAD)
    block_ones = jnp.where(same, 1.0, 0.0).astype(BF)

    def normed(x):
        x = x.astype(F32)
        return (x * lax.rsqrt(jnp.mean(x * x, axis=-1, keepdims=True) + EPS) * fine_gain).astype(BF)

    def cosine(x):
        total = mm((x * x).astype(BF), block_ones)
        return x * lax.rsqrt(total * (1.0 / HEAD) + EPS)

    factor = math.log2(math.e) / HEAD
    qscale = jnp.where(low, fscale_ref[0] * factor, fscale_ref[1] * factor)
    queries = cosine(mm(normed(image_ref[...]), fqkv_ref[:, 0:width])) * qscale
    qs[0] = jnp.where(low, queries, 0.0).astype(BF)
    qs[1] = jnp.where(low, 0.0, queries).astype(BF)
    slots[0] = image_ref[...]
    acc[...] = jnp.zeros_like(acc)

    pl.semaphore_wait(barrier, ndev - 1)

    def place(rc, bc):
        a = jnp.where(rc == 0, 0, jnp.where(rc == 1, sib, -sib))
        b = jnp.where(bc == 0, 0, jnp.where(bc == 1, -1, 1))
        r, c = row + a, col + b
        ok = (r >= 0) & (r < nrow) & (c >= 0) & (c < ncol)
        return r, c, ok

    def halo(rc, bc):
        r, c, ok = place(rc, bc)
        there = SWAP[bc] * 3 + rc
        copy = pltpu.make_async_remote_copy(
            src_ref=image_ref, dst_ref=slots.at[there], send_sem=hsend.at[bc * 3 + rc],
            recv_sem=hrecv.at[there], device_id={"row": r, "col": c}, device_id_type=MESH,
        )
        return copy, ok

    order = [(1, 0), (2, 0), (0, 1), (0, 2), (1, 1), (1, 2), (2, 1), (2, 2)]
    for rc, bc in order:
        copy, ok = halo(rc, bc)

        @pl.when(ok)
        def _():
            copy.start()

    def step(s, carry):
        _, _, ok = place(lax.rem(s, 3), s // 3)

        @pl.when(ok)
        def _():
            @pl.when(s > 0)
            def _():
                pltpu.make_async_remote_copy(
                    src_ref=image_ref, dst_ref=slots.at[s], send_sem=hsend.at[s],
                    recv_sem=hrecv.at[s], device_id={"row": row, "col": col}, device_id_type=MESH,
                ).wait_recv()

            proj = mm(normed(slots[s]), fqkv_ref[:, width:])
            keys = cosine(proj[:, 0:width])
            kt[...] = keys.T.astype(BF)
            values = proj[:, width:]
            vext[0] = jnp.where(low, values, 1.0).astype(BF)
            vext[1] = jnp.where(low, 1.0, values).astype(BF)

            def block(i, c2):
                rows = pl.ds(pl.multiple_of(i * QB, QB), QB)
                s0 = mm(qs[0, rows, :], kt[...])
                s1 = mm(qs[1, rows, :], kt[...])
                p0 = jnp.exp2(s0).astype(BF)
                acc[0, rows, :] += mm(p0, vext[0])
                p1 = jnp.exp2(s1).astype(BF)
                acc[1, rows, :] += mm(p1, vext[1])
                return c2

            lax.fori_loop(0, tokens // QB, block, 0)

        return carry

    lax.fori_loop(0, 9, step, 0)

    for load in loads:
        load.wait()
    coarse_gain = 1.0 + jnp.dot(cond, adac_w[...], precision=HIGHEST)[0:1]

    a0, a1 = acc[0], acc[1]
    num = jnp.where(low, a0, a1)
    den = pltpu.roll(jnp.where(low, a1, a0), HEAD, 1)
    attended = (num / den).astype(BF)
    branch = mm(attended, fout_ref[...])
    branch = branch * lax.rsqrt(jnp.mean(branch * branch, axis=-1, keepdims=True) + EPS)
    fine = (image_ref[...].astype(F32) + branch * fpost_ref[...]).astype(BF)
    fine_ref[...] = fine
    at = iota((64, tokens), 1)
    r, c = at // TILE, at % TILE
    span = 2 * POOL
    target = ((r % 2) * 2 + c % 2) * 16 + (r // span) * (TILE // span) + c // span
    pick = jnp.where(iota((64, tokens), 0) == target, 1.0, 0.0).astype(BF)
    sums = mm(pick, fine) * (1.0 / (POOL * POOL))
    high = sums.astype(BF)
    rest = (sums - high.astype(F32)).astype(BF)
    pooled = jnp.zeros((16, merge_w.shape[1]), F32)
    for p in range(4):
        part_w = merge_w[p * width : (p + 1) * width, :]
        pooled = pooled + mm(high[p * 16 : p * 16 + 16], part_w) + mm(rest[p * 16 : p * 16 + 16], part_w)
    coarse_in = mm(pooled.astype(BF), cin_w[...])
    cn = coarse_in * lax.rsqrt(jnp.mean(coarse_in * coarse_in, axis=-1, keepdims=True) + EPS) * coarse_gain
    quarter = coarse_in.shape[1] // 4
    for j in range(4):
        pack[4 * j : 4 * j + 4, :] = cn[0:4, j * quarter : (j + 1) * quarter]
    gath[me] = pack[...].astype(BF)

    def gather(i):
        peer = lax.rem(me + i, ndev)
        return pltpu.make_async_remote_copy(
            src_ref=gath.at[me], dst_ref=gath.at[me], send_sem=gsend.at[i], recv_sem=grecv.at[me],
            device_id={"row": peer // ncol, "col": lax.rem(peer, ncol)}, device_id_type=MESH,
        )

    def gather_from(i):
        peer = lax.rem(me + i, ndev)
        return pltpu.make_async_remote_copy(
            src_ref=gath.at[peer], dst_ref=gath.at[peer], send_sem=gsend.at[i],
            recv_sem=grecv.at[peer],
            device_id={"row": peer // ncol, "col": lax.rem(peer, ncol)}, device_id_type=MESH,
        )

    def loop(low_at, high_at, do):
        def one(i, carry):
            do(i)
            return carry

        lax.fori_loop(low_at, high_at, one, 0)

    loop(1, ndev, lambda i: gather(i).start())
    loop(1, ndev, lambda i: gather_from(i).wait_recv())

    every = gath[...].reshape(ndev * 16, quarter)
    lw = cqkv_w.shape[2]
    count = ndev * 4
    out_at, in_at = iota((count, ndev * 16), 0), iota((count, ndev * 16), 1)
    proj = [jnp.zeros((count, lw), F32) for _ in range(3)]
    for j in range(4):
        wanted = (out_at // 4) * 16 + j * 4 + out_at % 4
        chosen = mm(jnp.where(in_at == wanted, 1.0, 0.0).astype(BF), every).astype(BF)
        for k in range(3):
            proj[k] = proj[k] + mm(chosen, cqkv_w[k, j * quarter : (j + 1) * quarter, :])
    head_same = (iota((lw, lw), 0) // HEAD) == (iota((lw, lw), 1) // HEAD)
    head_ones = jnp.where(head_same, 1.0, 0.0)

    def ccosine(x):
        total = jnp.dot(x * x, head_ones, precision=HIGHEST)
        return x * lax.rsqrt(total * (1.0 / HEAD) + EPS)

    qall[...] = ccosine(proj[0])
    keys = ccosine(proj[1]).astype(BF)
    values = proj[2].astype(BF)
    own = ncol * 4
    queries = qall[pl.ds(pl.multiple_of(row * own, own), own), :]
    heads = lw // HEAD
    lane_head = iota((own, lw), 1) // HEAD
    stack = jnp.concatenate(
        [jnp.where(lane_head == h, queries, 0.0) for h in range(heads)], axis=0
    ).astype(BF)
    scores = lax.dot_general(stack, keys, (((1,), (1,)), ((), ())), preferred_element_type=F32)
    results = jnp.zeros((own, lw), F32)
    for h in range(heads):
        expo = jnp.exp(scores[h * own : (h + 1) * own] * (cscale_ref[h] / HEAD))
        weights = (expo / jnp.sum(expo, axis=-1, keepdims=True)).astype(BF)
        results = results + jnp.where(lane_head == h, mm(weights, values), 0.0)
    partial = mm(results.astype(BF), cout_w[...])
    for k in range(ncol):
        for j in range(4):
            pack[4 * j : 4 * j + 4, :] = partial[4 * k : 4 * k + 4, j * quarter : (j + 1) * quarter]
        sbuf[k] = pack[...].astype(BF)
    rbuf[col] = sbuf[col]

    def reduce(i):
        peer = lax.rem(col + i, ncol)
        return pltpu.make_async_remote_copy(
            src_ref=sbuf.at[peer], dst_ref=rbuf.at[col], send_sem=rsend.at[i],
            recv_sem=rrecv.at[col], device_id={"row": row, "col": peer}, device_id_type=MESH,
        )

    def reduce_from(i):
        peer = lax.rem(col + i, ncol)
        return pltpu.make_async_remote_copy(
            src_ref=sbuf.at[peer], dst_ref=rbuf.at[peer], send_sem=rsend.at[i],
            recv_sem=rrecv.at[peer], device_id={"row": row, "col": peer}, device_id_type=MESH,
        )

    loop(1, ncol, lambda i: reduce(i).start())
    loop(1, ncol, lambda i: reduce_from(i).wait_recv())
    total = jnp.sum(rbuf[...].astype(F32), axis=0)
    pack[...] = total
    pieces = [pack[4 * j : 4 * j + 4, :] for j in range(4)]
    power = sum(jnp.sum(piece * piece, axis=-1, keepdims=True) for piece in pieces)
    inverse = lax.rsqrt(power * (1.0 / (4 * quarter)) + EPS)
    for j in range(4):
        at_j = slice(j * quarter, (j + 1) * quarter)
        y = coarse_in[0:4, at_j] + pieces[j] * inverse * cpost_ref[:, at_j]
        coarse_ref[:, at_j] = y

    for rc, bc in order:
        copy, ok = halo(rc, bc)

        @pl.when(ok)
        def _():
            copy.wait_send()

    loop(1, ndev, lambda i: gather(i).wait_send())
    loop(1, ncol, lambda i: reduce(i).wait_send())


def body(
    image, noise_level, cond_table, ada_fine, fine_qkv, fine_scale, fine_out_w, fine_post,
    merge_w, coarse_in_w, ada_coarse, coarse_qkv, coarse_scale, coarse_out_w, coarse_post,
):
    nrow, ncol = lax.axis_size("row"), lax.axis_size("col")
    ndev = nrow * ncol
    rows, cols, width = image.shape
    tokens = rows * cols
    lw = coarse_qkv.shape[2]
    cw = coarse_in_w.shape[1]
    quarter = cw // 4
    smem = pl.BlockSpec(memory_space=pltpu.SMEM)
    vmem = pl.BlockSpec(memory_space=pltpu.VMEM)
    hbm = pl.BlockSpec(memory_space=pl.ANY)
    dma = pltpu.SemaphoreType.DMA
    fine, coarse = pl.pallas_call(
        functools.partial(kernel, nrow, ncol),
        out_shape=(
            jax.ShapeDtypeStruct((tokens, width), BF),
            jax.ShapeDtypeStruct((4, cw), F32),
        ),
        in_specs=[smem] * 3 + [vmem] * 7 + [hbm] * 5,
        out_specs=(vmem, vmem),
        scratch_shapes=[
            pltpu.VMEM((9, tokens, width), BF),
            pltpu.VMEM((2, tokens, width), BF),
            pltpu.VMEM((width, tokens), BF),
            pltpu.VMEM((2, tokens, width), BF),
            pltpu.VMEM((2, tokens, width), F32),
            pltpu.VMEM(merge_w.shape, BF),
            pltpu.VMEM(coarse_in_w.shape, BF),
            pltpu.VMEM(ada_coarse.shape, F32),
            pltpu.VMEM(coarse_qkv.shape, BF),
            pltpu.VMEM(coarse_out_w.shape, BF),
            pltpu.VMEM((ndev, 16, quarter), BF),
            pltpu.VMEM((16, quarter), F32),
            pltpu.VMEM((ndev * 4, lw), F32),
            pltpu.VMEM((ncol, 16, quarter), BF),
            pltpu.VMEM((ncol, 16, quarter), BF),
            dma((5,)), dma((9,)), dma((9,)), dma((ndev,)), dma((ndev,)), dma((ncol,)), dma((ncol,)),
        ],
        compiler_params=pltpu.CompilerParams(
            collective_id=0, has_side_effects=True, vmem_limit_bytes=48 * 1024 * 1024
        ),
        cost_estimate=pl.CostEstimate(
            flops=tokens * tokens * 9 * width * 4, bytes_accessed=8 << 20,
            transcendentals=tokens * tokens * 18,
        ),
    )(
        noise_level, fine_scale, coarse_scale, image.reshape(tokens, width), cond_table, ada_fine,
        fine_qkv, fine_out_w, fine_post.reshape(1, -1), coarse_post.reshape(1, -1), merge_w,
        coarse_in_w, ada_coarse, coarse_qkv, coarse_out_w,
    )
    side = TILE // (2 * POOL)
    return fine.reshape(rows, cols, width), coarse.astype(BF).reshape(side, side, cw)


def solution(mesh):
    in_specs = (
        P(("noise", "row"), "col", None),
        P("noise"),
        P(),
        P(),
        P(),
        P(),
        P(),
        P(),
        P(),
        P(),
        P(),
        P(None, None, "col"),
        P("col"),
        P("col", None),
        P(),
    )
    out_specs = (P(("noise", "row"), "col", None), P(("noise", "row"), "col", None))
    return jax.shard_map(body, mesh=mesh, in_specs=in_specs, out_specs=out_specs, check_vma=False)
```

time: 263 us -> 66.1 us (0.25)
  matrix products: 107 us -> 0 us
  Pallas kernels: 0 us -> 50.4 us
  blocking collectives: 49.9 us -> 0 us
  other arithmetic: 41.9 us -> 0.01 us
  waiting for transfers between devices: 26.4 us -> 0 us
  starting transfers between devices: 9.58 us -> 0 us
  local copies, waits for them, and re-layouts: 19.9 us -> 13.8 us
  between operations: 6.37 us -> 1.32 us
    dot_general x26 -> x0, matrix products: 107 us -> none  [the longest x8 56.8 us: attend(): jnp.dot(queries[:, low:low + HEAD], keys[:, low:low + HEAD].T, preferred_...]
    pallas_call x0 -> x1, Pallas kernels: none -> 50.4 us  [body(): pl.pallas_call(functools.partial(kernel, nrow, ncol), out_shape=(jax.Shap...]
    all_gather x1 -> x0, blocking collectives: 32.3 us -> none  [body(): lax.all_gather(cn, ('row', 'col'), axis=0, tiled=True)]
    reduce_sum x12 -> x0, other arithmetic: 29.1 us -> none  [the longest x6 24.2 us: attend(): jnp.sum(expo, axis=-1, keepdims=True)]
    ppermute x4 -> x0, waiting for transfers between devices: 26.4 us -> none  [the longest x2 16.1 us: with_halo(): before = lax.ppermute(last, axis, up)]
    unnamed x1 -> x0, blocking collectives: 17.6 us -> none
    unnamed x29, local copies, waits for them, and re-layouts: 1.73 us -> 13.2 us
    ppermute x4 -> x0, starting transfers between devices: 9.58 us -> none  [the longest x2 7.01 us: with_halo(): before = lax.ppermute(last, axis, up)]
  transfers between devices with their start and end apart: 4 -> 0, of which waited for: 4 -> 0; matrix products, arithmetic and copies ran while one was open for 2% -> 0% of each run, Pallas kernels for 0% -> 0%
where the time goes in v1:
time: 66.1 us; the launch traced here: 65.6 us
  Pallas kernels  50.4 us (76%)
  local copies, waits for them, and re-layouts  13.8 us (21%)
  between operations  1.32 us (2%)
    pallas_call x1, Pallas kernels, body(): pl.pallas_call(functools.partial(kernel, nrow, ncol), out_shape=(jax.Shap...  50.4 us
    unnamed x29, local copies, waits for them, and re-layouts  13.2 us

profile of v1, /device:TPU:0, one launch (start us, length us, event | category | flops | bytes accessed | tf_op | source)
XLA Modules:
  0.0 65.6 jit_solution(2487312314055030733)
XLA Ops:
  1.3 0.0 copy-start
  1.3 1.4 %copy-done = bf16[3,1024,256]{2,1,0:T(8,128)(2,1)S(1)} copy-done((bf16[3,1024,256]{2,1,0:T(8,128)(2,1)S(1)}, bf16[3,1024,256]{2,1,0:T(8,128)(2,1)}, u32[]{:S(2)}) %copy-start) | copy-done | bytes 1572888
  2.7 0.0 copy-start.1
  2.7 1.2 %copy-done.1 = f32[256,1024]{1,0:T(8,128)S(1)} copy-done((f32[256,1024]{1,0:T(8,128)S(1)}, f32[256,1024]{1,0:T(8,128)}, u32[]{:S(2)}) %copy-start.1) | copy-done | bytes 1048600
  3.9 0.0 copy-start.2
  3.9 1.0 %copy-done.2 = bf16[256,1024]{1,0:T(8,128)(2,1)S(1)} copy-done((bf16[256,1024]{1,0:T(8,128)(2,1)S(1)}, bf16[256,1024]{1,0:T(8,128)(2,1)}, u32[]{:S(2)}) %copy-start.2) | copy-done | bytes 524312
  5.0 0.0 copy-start.3
  5.0 1.0 %copy-done.3 = bf16[256,1024]{1,0:T(8,128)(2,1)S(1)} copy-done((bf16[256,1024]{1,0:T(8,128)(2,1)S(1)}, bf16[256,1024]{1,0:T(8,128)(2,1)}, u32[]{:S(2)}) %copy-start.3) | copy-done | bytes 524312
  6.0 0.0 copy-start.4
  6.0 0.9 %copy-done.4 = bf16[32,32,128]{2,1,0:T(8,128)(2,1)S(1)} copy-done((bf16[32,32,128]{2,1,0:T(8,128)(2,1)S(1)}, bf16[32,32,128]{2,1,0:T(8,128)(2,1)}, u32[]{:S(2)}) %copy-start.4) | copy-done | bytes 262168
  7.0 0.0 copy-start.5
  7.0 0.9 %copy-done.5 = bf16[512,256]{1,0:T(8,128)(2,1)S(1)} copy-done((bf16[512,256]{1,0:T(8,128)(2,1)S(1)}, bf16[512,256]{1,0:T(8,128)(2,1)}, u32[]{:S(2)}) %copy-start.5) | copy-done | bytes 262168
  7.9 0.0 copy-start.6
  7.9 0.9 %copy-done.6 = f32[256,128]{1,0:T(8,128)S(1)} copy-done((f32[256,128]{1,0:T(8,128)S(1)}, f32[256,128]{1,0:T(8,128)}, u32[]{:S(2)}) %copy-start.6) | copy-done | bytes 131096
  8.8 0.0 copy-start.7
  8.8 0.9 %copy-done.7 = bf16[128,384]{1,0:T(8,128)(2,1)S(1)} copy-done((bf16[128,384]{1,0:T(8,128)(2,1)S(1)}, bf16[128,384]{1,0:T(8,128)(2,1)}, u32[]{:S(2)}) %copy-start.7) | copy-done | bytes 98328
  9.7 0.0 copy-start.8
  9.7 0.8 %copy-done.8 = bf16[128,128]{1,0:T(8,128)(2,1)S(1)} copy-done((bf16[128,128]{1,0:T(8,128)(2,1)S(1)}, bf16[128,128]{1,0:T(8,128)(2,1)}, u32[]{:S(2)}) %copy-start.8) | copy-done | bytes 32792
  10.5 0.0 copy-start.9
  10.5 0.7 %copy-done.9 = f32[8,256]{1,0:T(8,128)S(1)} copy-done((f32[8,256]{1,0:T(8,128)S(1)}, f32[8,256]{1,0:T(8,128)}, u32[]{:S(2)}) %copy-start.9) | copy-done | bytes 8216
  11.2 0.0 copy-start.10
  11.2 0.7 %copy-done.10 = f32[1024]{0:T(1024)S(1)} copy-done((f32[1024]{0:T(1024)S(1)}, f32[1024]{0:T(1024)}, u32[]{:S(2)}) %copy-start.10) | copy-done | bytes 4120
  11.8 0.0 copy-start.11
  11.8 0.7 copy-done.11
  12.5 0.0 copy-start.12
  12.5 0.7 copy-done.12
  13.2 0.0 copy-start.13
  13.2 0.7 copy-done.13
  13.8 50.4 %shard_map.158 = (bf16[1024,128]{1,0:T(8,128)(2,1)S(1)}, f32[4,1024]{1,0:T(4,128)S(1)}) custom-call(s32[1]{0:T(128)S(6)} %copy.18.level_ref, f32[2]{0:T(128)S(1)} %copy-done.11, f32[4]{0:T(128)S(1)} %copy-done.12, bf16[1024,128]{1,0:T(8,128)(2,1)S(1)} %bitcast.5, f32[8,256]{1,0:T(8,128)S(1)} %copy-done.9, f32[256,128]{1,0:T(8,128)S(1)} %copy-done.6, ...), custom_call_target="tpu_custom_call" | custom-call | flops 4831838208 | bytes 8388608 | tf_op jit(solution)/shard_map/pallas_call | solution.py:299
  64.3 0.6 reshape.23
  64.9 0.7 %copy.19 = bf16[32,32,128]{2,1,0:T(8,128)(2,1)} copy(bf16[32,32,128]{2,1,0:T(8,128)(2,1)S(1)} %bitcast.4) | data formatting | bytes 524288
  (1 shorter events, 0.0 us)
Async XLA Ops:
  1.3 1.4 %copy-start = (bf16[3,1024,256]{2,1,0:T(8,128)(2,1)S(1)}, bf16[3,1024,256]{2,1,0:T(8,128)(2,1)}, u32[]{:S(2)}) copy-start(bf16[3,1024,256]{2,1,0:T(8,128)(2,1)} %cqkv_hbm.1) | copy-start | bytes 4718596
  2.7 1.2 %copy-start.1 = (f32[256,1024]{1,0:T(8,128)S(1)}, f32[256,1024]{1,0:T(8,128)}, u32[]{:S(2)}) copy-start(f32[256,1024]{1,0:T(8,128)} %adac_hbm.1) | copy-start | bytes 3145732
  3.9 1.0 %copy-start.2 = (bf16[256,1024]{1,0:T(8,128)(2,1)S(1)}, bf16[256,1024]{1,0:T(8,128)(2,1)}, u32[]{:S(2)}) copy-start(bf16[256,1024]{1,0:T(8,128)(2,1)} %cin_hbm.1) | copy-start | bytes 1572868
  5.0 1.0 %copy-start.3 = (bf16[256,1024]{1,0:T(8,128)(2,1)S(1)}, bf16[256,1024]{1,0:T(8,128)(2,1)}, u32[]{:S(2)}) copy-start(bf16[256,1024]{1,0:T(8,128)(2,1)} %cout_hbm.1) | copy-start | bytes 1572868
  6.0 0.9 %copy-start.4 = (bf16[32,32,128]{2,1,0:T(8,128)(2,1)S(1)}, bf16[32,32,128]{2,1,0:T(8,128)(2,1)}, u32[]{:S(2)}) copy-start(bf16[32,32,128]{2,1,0:T(8,128)(2,1)} %param.15) | copy-start | bytes 786436
  7.0 0.9 %copy-start.5 = (bf16[512,256]{1,0:T(8,128)(2,1)S(1)}, bf16[512,256]{1,0:T(8,128)(2,1)}, u32[]{:S(2)}) copy-start(bf16[512,256]{1,0:T(8,128)(2,1)} %merge_hbm.1) | copy-start | bytes 786436
  7.9 0.9 %copy-start.6 = (f32[256,128]{1,0:T(8,128)S(1)}, f32[256,128]{1,0:T(8,128)}, u32[]{:S(2)}) copy-start(f32[256,128]{1,0:T(8,128)} %ada_fine_ref.1) | copy-start | bytes 393220
  8.8 0.9 %copy-start.7 = (bf16[128,384]{1,0:T(8,128)(2,1)S(1)}, bf16[128,384]{1,0:T(8,128)(2,1)}, u32[]{:S(2)}) copy-start(bf16[128,384]{1,0:T(8,128)(2,1)} %fqkv_ref.1) | copy-start | bytes 294916
  9.7 0.8 %copy-start.8 = (bf16[128,128]{1,0:T(8,128)(2,1)S(1)}, bf16[128,128]{1,0:T(8,128)(2,1)}, u32[]{:S(2)}) copy-start(bf16[128,128]{1,0:T(8,128)(2,1)} %fout_ref.1) | copy-start | bytes 98308
  10.5 0.7 %copy-start.9 = (f32[8,256]{1,0:T(8,128)S(1)}, f32[8,256]{1,0:T(8,128)}, u32[]{:S(2)}) copy-start(f32[8,256]{1,0:T(8,128)} %table_ref.1) | copy-start | bytes 24580
  11.2 0.7 %copy-start.10 = (f32[1024]{0:T(1024)S(1)}, f32[1024]{0:T(1024)}, u32[]{:S(2)}) copy-start(f32[1024]{0:T(1024)} %param.29) | copy-start | bytes 12292
  11.8 0.7 copy-start.11
  12.5 0.7 copy-start.12
  13.2 0.7 copy-start.13

commit v2 on v1

--- a/solution.py
+++ b/solution.py
@@ -12,6 +12,7 @@
 TILE = 32
 POOL = 8
 QB = 256
+VMEM_BYTES = 64 * 1024 * 1024 - 65536
 EPS = 1e-6
 MESH = pl.DeviceIdType.MESH
 HIGHEST = lax.Precision.HIGHEST
@@ -29,17 +30,31 @@
 
 
 def kernel(
-    nrow, ncol, level_ref, fscale_ref, cscale_ref, image_ref, table_ref, ada_fine_ref, fqkv_ref,
-    fout_ref, fpost_ref, cpost_ref, merge_hbm, cin_hbm, adac_hbm, cqkv_hbm, cout_hbm,
-    fine_ref, coarse_ref,
-    slots, qs, kt, vext, acc, merge_w, cin_w, adac_w, cqkv_w, cout_w, gath, pack, qall,
+    nrow, ncol, level_ref, fscale_ref, cscale_ref, image_hbm, table_hbm, adaf_hbm, fqkv_hbm,
+    fout_hbm, fpost_hbm, cpost_hbm, merge_hbm, cin_hbm, adac_hbm, cqkv_hbm, cout_hbm,
+    fine_hbm, coarse_ref,
+    slots, qs, kt, vext, acc, table_ref, ada_fine_ref, fqkv_ref, fout_ref, fpost_ref, cpost_ref,
+    merge_w, cin_w, adac_w, cqkv_w, cout_w, fine_ref, gath, pack, qall,
     sbuf, rbuf, local_sem, hsend, hrecv, gsend, grecv, rsend, rrecv,
 ):
-    tokens, width = image_ref.shape
+    tokens, width = image_hbm.shape
+    image_ref = slots.at[0]
     ndev = nrow * ncol
     row, col = lax.axis_index("row"), lax.axis_index("col")
     me = row * ncol + col
     sib = 1 - 2 * lax.rem(row, 2)
+
+    loads = [
+        pltpu.make_async_copy(src, dst, local_sem.at[i])
+        for i, (src, dst) in enumerate(
+            ((image_hbm, image_ref), (table_hbm, table_ref), (adaf_hbm, ada_fine_ref),
+             (fqkv_hbm, fqkv_ref), (adac_hbm, adac_w), (fout_hbm, fout_ref),
+             (fpost_hbm, fpost_ref), (cpost_hbm, cpost_ref), (merge_hbm, merge_w),
+             (cin_hbm, cin_w), (cqkv_hbm, cqkv_w), (cout_hbm, cout_w))
+        )
+    ]
+    for load in loads:
+        load.start()
 
     barrier = pltpu.get_barrier_semaphore()
 
@@ -52,16 +67,8 @@
         return carry
 
     lax.fori_loop(1, ndev, greet, 0)
-    loads = [
-        pltpu.make_async_copy(src, dst, local_sem.at[i])
-        for i, (src, dst) in enumerate(
-            ((merge_hbm, merge_w), (cin_hbm, cin_w), (adac_hbm, adac_w), (cqkv_hbm, cqkv_w),
-             (cout_hbm, cout_w))
-        )
-    ]
-    for load in loads:
-        load.start()
-
+    for load in loads[:4]:
+        load.wait()
     levels = table_ref.shape[0]
     hot = iota((levels, 1), 0) == level_ref[0]
     cond = jnp.sum(jnp.where(hot, table_ref[...], 0.0), axis=0, keepdims=True)
@@ -81,11 +88,12 @@
 
     factor = math.log2(math.e) / HEAD
     qscale = jnp.where(low, fscale_ref[0] * factor, fscale_ref[1] * factor)
-    queries = cosine(mm(normed(image_ref[...]), fqkv_ref[:, 0:width])) * qscale
+    queries = cosine(mm(normed(slots[0]), fqkv_ref[:, 0:width])) * qscale
     qs[0] = jnp.where(low, queries, 0.0).astype(BF)
     qs[1] = jnp.where(low, 0.0, queries).astype(BF)
-    slots[0] = image_ref[...]
     acc[...] = jnp.zeros_like(acc)
+    loads[4].wait()
+    coarse_gain = 1.0 + jnp.dot(cond, adac_w[...], precision=HIGHEST)[0:1]
 
     pl.semaphore_wait(barrier, ndev - 1)
 
@@ -142,15 +150,14 @@
                 acc[1, rows, :] += mm(p1, vext[1])
                 return c2
 
-            lax.fori_loop(0, tokens // QB, block, 0)
+            lax.fori_loop(0, tokens // QB, block, 0, unroll=2)
 
         return carry
 
     lax.fori_loop(0, 9, step, 0)
 
-    for load in loads:
+    for load in loads[5:]:
         load.wait()
-    coarse_gain = 1.0 + jnp.dot(cond, adac_w[...], precision=HIGHEST)[0:1]
 
     a0, a1 = acc[0], acc[1]
     num = jnp.where(low, a0, a1)
@@ -158,8 +165,10 @@
     attended = (num / den).astype(BF)
     branch = mm(attended, fout_ref[...])
     branch = branch * lax.rsqrt(jnp.mean(branch * branch, axis=-1, keepdims=True) + EPS)
-    fine = (image_ref[...].astype(F32) + branch * fpost_ref[...]).astype(BF)
+    fine = (slots[0].astype(F32) + branch * fpost_ref[...]).astype(BF)
     fine_ref[...] = fine
+    store = pltpu.make_async_copy(fine_ref, fine_hbm, local_sem.at[len(loads)])
+    store.start()
     at = iota((64, tokens), 1)
     r, c = at // TILE, at % TILE
     span = 2 * POOL
@@ -268,7 +277,11 @@
     for j in range(4):
         at_j = slice(j * quarter, (j + 1) * quarter)
         y = coarse_in[0:4, at_j] + pieces[j] * inverse * cpost_ref[:, at_j]
-        coarse_ref[:, at_j] = y
+        for k in range(coarse_ref.shape[0]):
+            side = coarse_ref.shape[1]
+            coarse_ref[k, :, at_j] = y[k * side : (k + 1) * side].astype(BF)
+
+    store.wait()
 
     for rc, bc in order:
         copy, ok = halo(rc, bc)
@@ -292,6 +305,7 @@
     lw = coarse_qkv.shape[2]
     cw = coarse_in_w.shape[1]
     quarter = cw // 4
+    side = TILE // (2 * POOL)
     smem = pl.BlockSpec(memory_space=pltpu.SMEM)
     vmem = pl.BlockSpec(memory_space=pltpu.VMEM)
     hbm = pl.BlockSpec(memory_space=pl.ANY)
@@ -300,30 +314,37 @@
         functools.partial(kernel, nrow, ncol),
         out_shape=(
             jax.ShapeDtypeStruct((tokens, width), BF),
-            jax.ShapeDtypeStruct((4, cw), F32),
+            jax.ShapeDtypeStruct((side, side, cw), BF),
         ),
-        in_specs=[smem] * 3 + [vmem] * 7 + [hbm] * 5,
-        out_specs=(vmem, vmem),
+        in_specs=[smem] * 3 + [hbm] * 12,
+        out_specs=(hbm, vmem),
         scratch_shapes=[
             pltpu.VMEM((9, tokens, width), BF),
             pltpu.VMEM((2, tokens, width), BF),
             pltpu.VMEM((width, tokens), BF),
             pltpu.VMEM((2, tokens, width), BF),
             pltpu.VMEM((2, tokens, width), F32),
+            pltpu.VMEM(cond_table.shape, F32),
+            pltpu.VMEM(ada_fine.shape, F32),
+            pltpu.VMEM(fine_qkv.shape, BF),
+            pltpu.VMEM(fine_out_w.shape, BF),
+            pltpu.VMEM((1, width), F32),
+            pltpu.VMEM((1, cw), F32),
             pltpu.VMEM(merge_w.shape, BF),
             pltpu.VMEM(coarse_in_w.shape, BF),
             pltpu.VMEM(ada_coarse.shape, F32),
             pltpu.VMEM(coarse_qkv.shape, BF),
             pltpu.VMEM(coarse_out_w.shape, BF),
+            pltpu.VMEM((tokens, width), BF),
             pltpu.VMEM((ndev, 16, quarter), BF),
             pltpu.VMEM((16, quarter), F32),
             pltpu.VMEM((ndev * 4, lw), F32),
             pltpu.VMEM((ncol, 16, quarter), BF),
             pltpu.VMEM((ncol, 16, quarter), BF),
-            dma((5,)), dma((9,)), dma((9,)), dma((ndev,)), dma((ndev,)), dma((ncol,)), dma((ncol,)),
+            dma((13,)), dma((9,)), dma((9,)), dma((ndev,)), dma((ndev,)), dma((ncol,)), dma((ncol,)),
         ],
         compiler_params=pltpu.CompilerParams(
-            collective_id=0, has_side_effects=True, vmem_limit_bytes=48 * 1024 * 1024
+            collective_id=0, has_side_effects=True, vmem_limit_bytes=VMEM_BYTES
         ),
         cost_estimate=pl.CostEstimate(
             flops=tokens * tokens * 9 * width * 4, bytes_accessed=8 << 20,
@@ -334,8 +355,7 @@
         fine_qkv, fine_out_w, fine_post.reshape(1, -1), coarse_post.reshape(1, -1), merge_w,
         coarse_in_w, ada_coarse, coarse_qkv, coarse_out_w,
     )
-    side = TILE // (2 * POOL)
-    return fine.reshape(rows, cols, width), coarse.astype(BF).reshape(side, side, cw)
+    return fine.reshape(rows, cols, width), coarse
 
 
 def solution(mesh):

time: 66.1 us -> 54.2 us (0.82)
  local copies, waits for them, and re-layouts: 13.8 us -> 2.97 us
  Pallas kernels: 50.4 us -> 49.7 us
    unnamed x29 -> x2, local copies, waits for them, and re-layouts: 13.2 us -> 2.97 us
    pallas_call x1, Pallas kernels: 50.4 us -> 49.7 us  [body(): pl.pallas_call(functools.partial(kernel, nrow, ncol), out_shape=(jax.Shap...]
where the time goes in v2:
time: 54.2 us; the launch traced here: 54 us
  Pallas kernels  49.7 us (92%)
  local copies, waits for them, and re-layouts  2.97 us (5%)
  between operations  1.29 us (2%)
    pallas_call x1, Pallas kernels, body(): pl.pallas_call(functools.partial(kernel, nrow, ncol), out_shape=(jax.Shap...  49.7 us
    unnamed x2, local copies, waits for them, and re-layouts  2.97 us

profile of v2, /device:TPU:0, one launch (start us, length us, event | category | flops | bytes accessed | tf_op | source)
XLA Modules:
  0.0 54.0 jit_solution(16110423969392080911)
XLA Ops:
  1.3 49.7 %shard_map.158 = (bf16[1024,128]{1,0:T(8,128)(2,1)}, bf16[2,2,1024]{2,1,0:T(2,128)(2,1)}) custom-call(s32[1]{0:T(128)S(6)} %copy.19.level_ref, f32[2]{0:T(128)} %fscale_ref.1, f32[4]{0:T(128)} %cscale_ref.1, bf16[1024,128]{1,0:T(8,128)(2,1)} %bitcast.5, f32[8,256]{1,0:T(8,128)} %table_hbm.1, f32[256,128]{1,0:T(8,128)} %adaf_hbm.1, ...), custom_call_target="tpu_custom_call" | custom-call | flops 4831838208 | bytes 8388608 | tf_op jit(solution)/shard_map/pallas_call | solution.py:313
  51.0 1.7 %copy.20 = bf16[32,32,128]{2,1,0:T(8,128)(2,1)} copy(bf16[32,32,128]{2,1,0:T(8,128)(2,1)} %bitcast.4) | data formatting | bytes 524288
  52.6 1.3 %copy.21 = bf16[2,2,1024]{2,1,0:T(2,128)(2,1)} copy(bf16[2,2,1024]{2,1,0:T(2,128)(2,1)} %get-tuple-element.9) | data formatting | bytes 16384

commit v3 on v2

--- a/solution.py
+++ b/solution.py
@@ -11,7 +11,7 @@
 HEAD = 64
 TILE = 32
 POOL = 8
-QB = 256
+KB = 256
 VMEM_BYTES = 64 * 1024 * 1024 - 65536
 EPS = 1e-6
 MESH = pl.DeviceIdType.MESH
@@ -78,9 +78,12 @@
     same = (iota((width, width), 0) // HEAD) == (iota((width, width), 1) // HEAD)
     block_ones = jnp.where(same, 1.0, 0.0).astype(BF)
 
+    all_ones = jnp.ones((width, width), BF)
+
     def normed(x):
         x = x.astype(F32)
-        return (x * lax.rsqrt(jnp.mean(x * x, axis=-1, keepdims=True) + EPS) * fine_gain).astype(BF)
+        total = mm((x * x).astype(BF), all_ones)
+        return (x * lax.rsqrt(total * (1.0 / width) + EPS) * fine_gain).astype(BF)
 
     def cosine(x):
         total = mm((x * x).astype(BF), block_ones)
@@ -135,22 +138,21 @@
 
             proj = mm(normed(slots[s]), fqkv_ref[:, width:])
             keys = cosine(proj[:, 0:width])
-            kt[...] = keys.T.astype(BF)
+            for i in range(tokens // KB):
+                kt[i] = keys[i * KB : (i + 1) * KB].T.astype(BF)
             values = proj[:, width:]
             vext[0] = jnp.where(low, values, 1.0).astype(BF)
             vext[1] = jnp.where(low, 1.0, values).astype(BF)
 
             def block(i, c2):
-                rows = pl.ds(pl.multiple_of(i * QB, QB), QB)
-                s0 = mm(qs[0, rows, :], kt[...])
-                s1 = mm(qs[1, rows, :], kt[...])
-                p0 = jnp.exp2(s0).astype(BF)
-                acc[0, rows, :] += mm(p0, vext[0])
-                p1 = jnp.exp2(s1).astype(BF)
-                acc[1, rows, :] += mm(p1, vext[1])
+                keys_at = pl.ds(pl.multiple_of(i * KB, KB), KB)
+                for head in range(2):
+                    scores = mm(qs[head], kt[i])
+                    expo = jnp.exp2(scores).astype(BF)
+                    acc[head] += mm(expo, vext[head, keys_at, :])
                 return c2
 
-            lax.fori_loop(0, tokens // QB, block, 0, unroll=2)
+            lax.fori_loop(0, tokens // KB, block, 0)
 
         return carry
 
@@ -294,6 +296,17 @@
     loop(1, ncol, lambda i: reduce(i).wait_send())
 
 
+def writer(fine_ref, coarse_ref, fine_out_ref, coarse_out_ref, sem):
+    copies = [
+        pltpu.make_async_copy(fine_ref, fine_out_ref, sem.at[0]),
+        pltpu.make_async_copy(coarse_ref, coarse_out_ref, sem.at[1]),
+    ]
+    for copy in copies:
+        copy.start()
+    for copy in copies:
+        copy.wait()
+
+
 def body(
     image, noise_level, cond_table, ada_fine, fine_qkv, fine_scale, fine_out_w, fine_post,
     merge_w, coarse_in_w, ada_coarse, coarse_qkv, coarse_scale, coarse_out_w, coarse_post,
@@ -321,7 +334,7 @@
         scratch_shapes=[
             pltpu.VMEM((9, tokens, width), BF),
             pltpu.VMEM((2, tokens, width), BF),
-            pltpu.VMEM((width, tokens), BF),
+            pltpu.VMEM((tokens // KB, width, KB), BF),
             pltpu.VMEM((2, tokens, width), BF),
             pltpu.VMEM((2, tokens, width), F32),
             pltpu.VMEM(cond_table.shape, F32),
@@ -355,6 +368,17 @@
         fine_qkv, fine_out_w, fine_post.reshape(1, -1), coarse_post.reshape(1, -1), merge_w,
         coarse_in_w, ada_coarse, coarse_qkv, coarse_out_w,
     )
+    fine, coarse = pl.pallas_call(
+        writer,
+        out_shape=(
+            jax.ShapeDtypeStruct(fine.shape, BF),
+            jax.ShapeDtypeStruct(coarse.shape, BF),
+        ),
+        in_specs=[hbm, hbm],
+        out_specs=(hbm, hbm),
+        scratch_shapes=[dma((2,))],
+        compiler_params=pltpu.CompilerParams(vmem_limit_bytes=VMEM_BYTES),
+    )(fine, coarse)
     return fine.reshape(rows, cols, width), coarse
 
 

time: 54.2 us -> 64.3 us (1.19)
  Pallas kernels: 49.7 us -> 62.9 us
  local copies, waits for them, and re-layouts: 2.97 us -> 0 us
    pallas_call x0 -> x1, Pallas kernels: none -> 9.31 us  [body(): pl.pallas_call(writer, out_shape=(jax.ShapeDtypeStruct(fine.shape, BF), j...]
    pallas_call x1, Pallas kernels: 49.7 us -> 53.6 us  [body(): pl.pallas_call(functools.partial(kernel, nrow, ncol), out_shape=(jax.Shap...]
    unnamed x2 -> x0, local copies, waits for them, and re-layouts: 2.97 us -> none
where the time goes in v3:
time: 64.3 us; the launch traced here: 64.2 us
  Pallas kernels  62.9 us (98%)
  between operations  1.29 us (2%)
    pallas_call x1, Pallas kernels, body(): pl.pallas_call(functools.partial(kernel, nrow, ncol), out_shape=(jax.Shap...  53.6 us
    pallas_call x1, Pallas kernels, body(): pl.pallas_call(writer, out_shape=(jax.ShapeDtypeStruct(fine.shape, BF), j...  9.31 us

profile of v3, /device:TPU:0, one launch (start us, length us, event | category | flops | bytes accessed | tf_op | source)
XLA Modules:
  0.0 64.2 jit_solution(622132276089375121)
XLA Ops:
  1.3 53.6 %shard_map.158 = (bf16[1024,128]{1,0:T(8,128)(2,1)}, bf16[2,2,1024]{2,1,0:T(2,128)(2,1)}) custom-call(s32[1]{0:T(128)S(6)} %copy.17.level_ref, f32[2]{0:T(128)} %fscale_ref.1, f32[4]{0:T(128)} %cscale_ref.1, bf16[1024,128]{1,0:T(8,128)(2,1)} %bitcast.4, f32[8,256]{1,0:T(8,128)} %table_hbm.1, f32[256,128]{1,0:T(8,128)} %adaf_hbm.1, ...), custom_call_target="tpu_custom_call" | custom-call | flops 4831838208 | bytes 8388608 | tf_op jit(solution)/shard_map/pallas_call | solution.py:326
  54.8 9.3 %shard_map.159 = (bf16[1024,128]{1,0:T(8,128)(2,1)}, bf16[2,2,1024]{2,1,0:T(2,128)(2,1)}) custom-call(bf16[1024,128]{1,0:T(8,128)(2,1)} %get-tuple-element.6.fine_ref, bf16[2,2,1024]{2,1,0:T(2,128)(2,1)} %get-tuple-element.7.coarse_ref), custom_call_target="tpu_custom_call" | custom-call | tf_op jit(solution)/shard_map/pallas_call | solution.py:371

commit v4 on v3

--- a/solution.py
+++ b/solution.py
@@ -12,6 +12,8 @@
 TILE = 32
 POOL = 8
 KB = 256
+QB = 256
+ROWS = HEAD + 16
 VMEM_BYTES = 64 * 1024 * 1024 - 65536
 EPS = 1e-6
 MESH = pl.DeviceIdType.MESH
@@ -92,8 +94,12 @@
     factor = math.log2(math.e) / HEAD
     qscale = jnp.where(low, fscale_ref[0] * factor, fscale_ref[1] * factor)
     queries = cosine(mm(normed(slots[0]), fqkv_ref[:, 0:width])) * qscale
-    qs[0] = jnp.where(low, queries, 0.0).astype(BF)
-    qs[1] = jnp.where(low, 0.0, queries).astype(BF)
+    first = iota((width, 1), 0) < HEAD
+    for i in range(tokens // QB):
+        part = queries[i * QB : (i + 1) * QB].T
+        qs[0, i] = jnp.where(first, part, 0.0).astype(BF)
+        qs[1, i] = jnp.where(first, 0.0, part).astype(BF)
+    vext[...] = jnp.ones_like(vext)
     acc[...] = jnp.zeros_like(acc)
     loads[4].wait()
     coarse_gain = 1.0 + jnp.dot(cond, adac_w[...], precision=HIGHEST)[0:1]
@@ -137,22 +143,24 @@
                 ).wait_recv()
 
             proj = mm(normed(slots[s]), fqkv_ref[:, width:])
-            keys = cosine(proj[:, 0:width])
+            kt[...] = cosine(proj[:, 0:width]).astype(BF)
             for i in range(tokens // KB):
-                kt[i] = keys[i * KB : (i + 1) * KB].T.astype(BF)
-            values = proj[:, width:]
-            vext[0] = jnp.where(low, values, 1.0).astype(BF)
-            vext[1] = jnp.where(low, 1.0, values).astype(BF)
+                at_i = slice(i * KB, (i + 1) * KB)
+                part = proj[at_i, width:].T.astype(BF)
+                for head in range(2):
+                    vext[head, 0:HEAD, at_i] = part[head * HEAD : (head + 1) * HEAD]
 
             def block(i, c2):
-                keys_at = pl.ds(pl.multiple_of(i * KB, KB), KB)
                 for head in range(2):
-                    scores = mm(qs[head], kt[i])
-                    expo = jnp.exp2(scores).astype(BF)
-                    acc[head] += mm(expo, vext[head, keys_at, :])
+                    total = acc[head, i]
+                    for j in range(tokens // KB):
+                        at_j = slice(j * KB, (j + 1) * KB)
+                        expo = jnp.exp2(mm(kt[at_j], qs[head, i])).astype(BF)
+                        total = total + mm(vext[head, :, at_j], expo)
+                    acc[head, i] = total
                 return c2
 
-            lax.fori_loop(0, tokens // KB, block, 0)
+            lax.fori_loop(0, tokens // QB, block, 0)
 
         return carry
 
@@ -161,10 +169,11 @@
     for load in loads[5:]:
         load.wait()
 
-    a0, a1 = acc[0], acc[1]
-    num = jnp.where(low, a0, a1)
-    den = pltpu.roll(jnp.where(low, a1, a0), HEAD, 1)
-    attended = (num / den).astype(BF)
+    parts = []
+    for i in range(tokens // QB):
+        ratio = [acc[head, i, 0:HEAD] / acc[head, i, HEAD : HEAD + 1] for head in range(2)]
+        parts.append(jnp.concatenate(ratio, axis=0).T.astype(BF))
+    attended = jnp.concatenate(parts, axis=0)
     branch = mm(attended, fout_ref[...])
     branch = branch * lax.rsqrt(jnp.mean(branch * branch, axis=-1, keepdims=True) + EPS)
     fine = (slots[0].astype(F32) + branch * fpost_ref[...]).astype(BF)
@@ -333,10 +342,10 @@
         out_specs=(hbm, vmem),
         scratch_shapes=[
             pltpu.VMEM((9, tokens, width), BF),
-            pltpu.VMEM((2, tokens, width), BF),
-            pltpu.VMEM((tokens // KB, width, KB), BF),
-            pltpu.VMEM((2, tokens, width), BF),
-            pltpu.VMEM((2, tokens, width), F32),
+            pltpu.VMEM((2, tokens // QB, width, QB), BF),
+            pltpu.VMEM((tokens, width), BF),
+            pltpu.VMEM((2, ROWS, tokens), BF),
+            pltpu.VMEM((2, tokens // QB, ROWS, QB), F32),
             pltpu.VMEM(cond_table.shape, F32),
             pltpu.VMEM(ada_fine.shape, F32),
             pltpu.VMEM(fine_qkv.shape, BF),

time: 64.3 us -> 75.6 us (1.18)
  Pallas kernels: 62.9 us -> 74.2 us
    pallas_call x1, Pallas kernels: 53.6 us -> 64.9 us  [body(): pl.pallas_call(functools.partial(kernel, nrow, ncol), out_shape=(jax.Shap...]
where the time goes in v4:
time: 75.6 us; the launch traced here: 75.5 us
  Pallas kernels  74.2 us (98%)
  between operations  1.29 us (2%)
    pallas_call x1, Pallas kernels, body(): pl.pallas_call(functools.partial(kernel, nrow, ncol), out_shape=(jax.Shap...  64.9 us
    pallas_call x1, Pallas kernels, body(): pl.pallas_call(writer, out_shape=(jax.ShapeDtypeStruct(fine.shape, BF), j...  9.31 us

profile of v4, /device:TPU:0, one launch (start us, length us, event | category | flops | bytes accessed | tf_op | source)
XLA Modules:
  0.0 75.5 jit_solution(13526739432003162213)
XLA Ops:
  1.3 64.9 %shard_map.158 = (bf16[1024,128]{1,0:T(8,128)(2,1)}, bf16[2,2,1024]{2,1,0:T(2,128)(2,1)}) custom-call(s32[1]{0:T(128)S(6)} %copy.17.level_ref, f32[2]{0:T(128)} %fscale_ref.1, f32[4]{0:T(128)} %cscale_ref.1, bf16[1024,128]{1,0:T(8,128)(2,1)} %bitcast.4, f32[8,256]{1,0:T(8,128)} %table_hbm.1, f32[256,128]{1,0:T(8,128)} %adaf_hbm.1, ...), custom_call_target="tpu_custom_call" | custom-call | flops 4831838208 | bytes 8388608 | tf_op jit(solution)/shard_map/pallas_call | solution.py:335
  66.1 9.3 %shard_map.159 = (bf16[1024,128]{1,0:T(8,128)(2,1)}, bf16[2,2,1024]{2,1,0:T(2,128)(2,1)}) custom-call(bf16[1024,128]{1,0:T(8,128)(2,1)} %get-tuple-element.6.fine_ref, bf16[2,2,1024]{2,1,0:T(2,128)(2,1)} %get-tuple-element.7.coarse_ref), custom_call_target="tpu_custom_call" | custom-call | tf_op jit(solution)/shard_map/pallas_call | solution.py:380

commit v5 on v2

--- a/solution.py
+++ b/solution.py
@@ -11,7 +11,7 @@
 HEAD = 64
 TILE = 32
 POOL = 8
-QB = 256
+QB = 512
 VMEM_BYTES = 64 * 1024 * 1024 - 65536
 EPS = 1e-6
 MESH = pl.DeviceIdType.MESH
@@ -33,9 +33,9 @@
     nrow, ncol, level_ref, fscale_ref, cscale_ref, image_hbm, table_hbm, adaf_hbm, fqkv_hbm,
     fout_hbm, fpost_hbm, cpost_hbm, merge_hbm, cin_hbm, adac_hbm, cqkv_hbm, cout_hbm,
     fine_hbm, coarse_ref,
-    slots, qs, kt, vext, acc, table_ref, ada_fine_ref, fqkv_ref, fout_ref, fpost_ref, cpost_ref,
+    slots, qs, kt, vext, acc, acc_in, table_ref, ada_fine_ref, fqkv_ref, fout_ref, fpost_ref, cpost_ref,
     merge_w, cin_w, adac_w, cqkv_w, cout_w, fine_ref, gath, pack, qall,
-    sbuf, rbuf, local_sem, hsend, hrecv, gsend, grecv, rsend, rrecv,
+    sbuf, rbuf, local_sem, hsend, hrecv, gsend, grecv, rsend, rrecv, asend, arecv,
 ):
     tokens, width = image_hbm.shape
     image_ref = slots.at[0]
@@ -78,9 +78,12 @@
     same = (iota((width, width), 0) // HEAD) == (iota((width, width), 1) // HEAD)
     block_ones = jnp.where(same, 1.0, 0.0).astype(BF)
 
+    all_ones = jnp.ones((width, width), BF)
+
     def normed(x):
         x = x.astype(F32)
-        return (x * lax.rsqrt(jnp.mean(x * x, axis=-1, keepdims=True) + EPS) * fine_gain).astype(BF)
+        total = mm((x * x).astype(BF), all_ones)
+        return (x * lax.rsqrt(total * (1.0 / width) + EPS) * fine_gain).astype(BF)
 
     def cosine(x):
         total = mm((x * x).astype(BF), block_ones)
@@ -88,9 +91,13 @@
 
     factor = math.log2(math.e) / HEAD
     qscale = jnp.where(low, fscale_ref[0] * factor, fscale_ref[1] * factor)
-    queries = cosine(mm(normed(slots[0]), fqkv_ref[:, 0:width])) * qscale
-    qs[0] = jnp.where(low, queries, 0.0).astype(BF)
-    qs[1] = jnp.where(low, 0.0, queries).astype(BF)
+
+    def make_queries(owner, slot):
+        queries = cosine(mm(normed(slots[slot]), fqkv_ref[:, 0:width])) * qscale
+        qs[owner, 0] = jnp.where(low, queries, 0.0).astype(BF)
+        qs[owner, 1] = jnp.where(low, 0.0, queries).astype(BF)
+
+    make_queries(0, 0)
     acc[...] = jnp.zeros_like(acc)
     loads[4].wait()
     coarse_gain = 1.0 + jnp.dot(cond, adac_w[...], precision=HIGHEST)[0:1]
@@ -104,8 +111,17 @@
         ok = (r >= 0) & (r < nrow) & (c >= 0) & (c < ncol)
         return r, c, ok
 
+    def edge(r):
+        return (r == 0) | (r == nrow - 1)
+
+    shares = nrow > 2
+    helper, helped = shares & edge(row), shares & edge(row + sib)
+    blocks = tokens // QB
+
     def halo(rc, bc):
         r, c, ok = place(rc, bc)
+        if (rc, bc) == (1, 2):
+            ok = ok & jnp.logical_not(helper)
         there = SWAP[bc] * 3 + rc
         copy = pltpu.make_async_remote_copy(
             src_ref=image_ref, dst_ref=slots.at[there], send_sem=hsend.at[bc * 3 + rc],
@@ -121,8 +137,14 @@
         def _():
             copy.start()
 
+    assist = pltpu.make_async_remote_copy(
+        src_ref=acc.at[1], dst_ref=acc_in, send_sem=asend, recv_sem=arecv,
+        device_id={"row": row + sib, "col": col}, device_id_type=MESH,
+    )
+
     def step(s, carry):
         _, _, ok = place(lax.rem(s, 3), s // 3)
+        ok = ok & jnp.logical_not(helped & (s == 4))
 
         @pl.when(ok)
         def _():
@@ -140,26 +162,46 @@
             vext[0] = jnp.where(low, values, 1.0).astype(BF)
             vext[1] = jnp.where(low, 1.0, values).astype(BF)
 
-            def block(i, c2):
-                rows = pl.ds(pl.multiple_of(i * QB, QB), QB)
-                s0 = mm(qs[0, rows, :], kt[...])
-                s1 = mm(qs[1, rows, :], kt[...])
-                p0 = jnp.exp2(s0).astype(BF)
-                acc[0, rows, :] += mm(p0, vext[0])
-                p1 = jnp.exp2(s1).astype(BF)
-                acc[1, rows, :] += mm(p1, vext[1])
-                return c2
-
-            lax.fori_loop(0, tokens // QB, block, 0, unroll=2)
+            @pl.when(helper & (s == 1))
+            def _():
+                make_queries(1, 1)
+
+            def blocks_of(owner):
+                def block(i, c2):
+                    rows = pl.ds(pl.multiple_of(i * QB, QB), QB)
+                    s0 = mm(qs[owner, 0, rows, :], kt[...])
+                    s1 = mm(qs[owner, 1, rows, :], kt[...])
+                    p0 = jnp.exp2(s0).astype(BF)
+                    acc[owner, 0, rows, :] += mm(p0, vext[0])
+                    p1 = jnp.exp2(s1).astype(BF)
+                    acc[owner, 1, rows, :] += mm(p1, vext[1])
+                    return c2
+
+                return block
+
+            lax.fori_loop(jnp.where(helped & (s == 7), blocks // 2, 0), blocks, blocks_of(0), 0)
+            if shares:
+                extra = jnp.where(s == 3, blocks, jnp.where(s == 6, blocks // 2, 0))
+                lax.fori_loop(0, jnp.where(helper, extra, 0), blocks_of(1), 0)
+
+        if shares:
+            @pl.when(helper & (s == 6))
+            def _():
+                assist.start()
 
         return carry
 
     lax.fori_loop(0, 9, step, 0)
+    if shares:
+        @pl.when(helped)
+        def _():
+            assist.wait_recv()
+            acc[0] += acc_in[...]
 
     for load in loads[5:]:
         load.wait()
 
-    a0, a1 = acc[0], acc[1]
+    a0, a1 = acc[0, 0], acc[0, 1]
     num = jnp.where(low, a0, a1)
     den = pltpu.roll(jnp.where(low, a1, a0), HEAD, 1)
     attended = (num / den).astype(BF)
@@ -283,6 +325,11 @@
 
     store.wait()
 
+    if shares:
+        @pl.when(helper)
+        def _():
+            assist.wait_send()
+
     for rc, bc in order:
         copy, ok = halo(rc, bc)
 
@@ -320,9 +367,10 @@
         out_specs=(hbm, vmem),
         scratch_shapes=[
             pltpu.VMEM((9, tokens, width), BF),
-            pltpu.VMEM((2, tokens, width), BF),
+            pltpu.VMEM((2, 2, tokens, width), BF),
             pltpu.VMEM((width, tokens), BF),
             pltpu.VMEM((2, tokens, width), BF),
+            pltpu.VMEM((2, 2, tokens, width), F32),
             pltpu.VMEM((2, tokens, width), F32),
             pltpu.VMEM(cond_table.shape, F32),
             pltpu.VMEM(ada_fine.shape, F32),
@@ -342,6 +390,7 @@
             pltpu.VMEM((ncol, 16, quarter), BF),
             pltpu.VMEM((ncol, 16, quarter), BF),
             dma((13,)), dma((9,)), dma((9,)), dma((ndev,)), dma((ndev,)), dma((ncol,)), dma((ncol,)),
+            dma, dma,
         ],
         compiler_params=pltpu.CompilerParams(
             collective_id=0, has_side_effects=True, vmem_limit_bytes=VMEM_BYTES

time: 54.2 us -> 49.6 us (0.915)
  Pallas kernels: 49.7 us -> 45.1 us
    pallas_call x1, Pallas kernels: 49.7 us -> 45.1 us  [body(): pl.pallas_call(functools.partial(kernel, nrow, ncol), out_shape=(jax.Shap...]
where the time goes in v5:
time: 49.6 us; the launch traced here: 49.3 us
  Pallas kernels  45.1 us (91%)
  local copies, waits for them, and re-layouts  2.97 us (6%)
  between operations  1.29 us (3%)
    pallas_call x1, Pallas kernels, body(): pl.pallas_call(functools.partial(kernel, nrow, ncol), out_shape=(jax.Shap...  45.1 us
    unnamed x2, local copies, waits for them, and re-layouts  2.97 us

profile of v5, /device:TPU:0, one launch (start us, length us, event | category | flops | bytes accessed | tf_op | source)
XLA Modules:
  0.0 49.3 jit_solution(1211100565713864297)
XLA Ops:
  1.3 45.1 %shard_map.158 = (bf16[1024,128]{1,0:T(8,128)(2,1)}, bf16[2,2,1024]{2,1,0:T(2,128)(2,1)}) custom-call(s32[1]{0:T(128)S(6)} %copy.19.level_ref, f32[2]{0:T(128)} %fscale_ref.1, f32[4]{0:T(128)} %cscale_ref.1, bf16[1024,128]{1,0:T(8,128)(2,1)} %bitcast.5, f32[8,256]{1,0:T(8,128)} %table_hbm.1, f32[256,128]{1,0:T(8,128)} %adaf_hbm.1, ...), custom_call_target="tpu_custom_call" | custom-call | flops 4831838208 | bytes 8388608 | tf_op jit(solution)/shard_map/pallas_call | solution.py:360
  46.4 1.7 %copy.20 = bf16[32,32,128]{2,1,0:T(8,128)(2,1)} copy(bf16[32,32,128]{2,1,0:T(8,128)(2,1)} %bitcast.4) | data formatting | bytes 524288
  48.0 1.3 %copy.21 = bf16[2,2,1024]{2,1,0:T(2,128)(2,1)} copy(bf16[2,2,1024]{2,1,0:T(2,128)(2,1)} %get-tuple-element.9) | data formatting | bytes 16384

commit v6 on v5

--- a/solution.py
+++ b/solution.py
@@ -171,9 +171,9 @@
                     rows = pl.ds(pl.multiple_of(i * QB, QB), QB)
                     s0 = mm(qs[owner, 0, rows, :], kt[...])
                     s1 = mm(qs[owner, 1, rows, :], kt[...])
-                    p0 = jnp.exp2(s0).astype(BF)
+                    p0 = jnp.exp2(s0.astype(BF))
                     acc[owner, 0, rows, :] += mm(p0, vext[0])
-                    p1 = jnp.exp2(s1).astype(BF)
+                    p1 = jnp.exp2(s1.astype(BF))
                     acc[owner, 1, rows, :] += mm(p1, vext[1])
                     return c2
 

time: 49.6 us -> 49.7 us (level)
  no operation moved by 1% of the time
where the time goes in v6:
time: 49.7 us; the launch traced here: 49.5 us
  Pallas kernels  45.2 us (91%)
  local copies, waits for them, and re-layouts  2.97 us (6%)
  between operations  1.29 us (3%)
    pallas_call x1, Pallas kernels, body(): pl.pallas_call(functools.partial(kernel, nrow, ncol), out_shape=(jax.Shap...  45.2 us
    unnamed x2, local copies, waits for them, and re-layouts  2.97 us

profile of v6, /device:TPU:0, one launch (start us, length us, event | category | flops | bytes accessed | tf_op | source)
XLA Modules:
  0.0 49.5 jit_solution(631274320721881791)
XLA Ops:
  1.3 45.2 %shard_map.158 = (bf16[1024,128]{1,0:T(8,128)(2,1)}, bf16[2,2,1024]{2,1,0:T(2,128)(2,1)}) custom-call(s32[1]{0:T(128)S(6)} %copy.19.level_ref, f32[2]{0:T(128)} %fscale_ref.1, f32[4]{0:T(128)} %cscale_ref.1, bf16[1024,128]{1,0:T(8,128)(2,1)} %bitcast.5, f32[8,256]{1,0:T(8,128)} %table_hbm.1, f32[256,128]{1,0:T(8,128)} %adaf_hbm.1, ...), custom_call_target="tpu_custom_call" | custom-call | flops 4831838208 | bytes 8388608 | tf_op jit(solution)/shard_map/pallas_call | solution.py:360
  46.5 1.7 %copy.20 = bf16[32,32,128]{2,1,0:T(8,128)(2,1)} copy(bf16[32,32,128]{2,1,0:T(8,128)(2,1)} %bitcast.4) | data formatting | bytes 524288
  48.2 1.3 %copy.21 = bf16[2,2,1024]{2,1,0:T(2,128)(2,1)} copy(bf16[2,2,1024]{2,1,0:T(2,128)(2,1)} %get-tuple-element.9) | data formatting | bytes 16384

commit v7 on v5

--- a/solution.py
+++ b/solution.py
@@ -15,7 +15,6 @@
 VMEM_BYTES = 64 * 1024 * 1024 - 65536
 EPS = 1e-6
 MESH = pl.DeviceIdType.MESH
-HIGHEST = lax.Precision.HIGHEST
 BF = jnp.bfloat16
 F32 = jnp.float32
 SWAP = (0, 2, 1)
@@ -72,8 +71,8 @@
     levels = table_ref.shape[0]
     hot = iota((levels, 1), 0) == level_ref[0]
     cond = jnp.sum(jnp.where(hot, table_ref[...], 0.0), axis=0, keepdims=True)
-    cond = jnp.broadcast_to(cond, (8, cond.shape[1]))
-    fine_gain = 1.0 + jnp.dot(cond, ada_fine_ref[...], precision=HIGHEST)[0:1]
+    cond = jnp.broadcast_to(cond, (8, cond.shape[1])).T[:, 0:1]
+    fine_gain = 1.0 + jnp.sum(cond * ada_fine_ref[...], axis=0, keepdims=True)
     low = iota((1, width), 1) < HEAD
     same = (iota((width, width), 0) // HEAD) == (iota((width, width), 1) // HEAD)
     block_ones = jnp.where(same, 1.0, 0.0).astype(BF)
@@ -100,7 +99,7 @@
     make_queries(0, 0)
     acc[...] = jnp.zeros_like(acc)
     loads[4].wait()
-    coarse_gain = 1.0 + jnp.dot(cond, adac_w[...], precision=HIGHEST)[0:1]
+    coarse_gain = 1.0 + jnp.sum(cond * adac_w[...], axis=0, keepdims=True)
 
     pl.semaphore_wait(barrier, ndev - 1)
 
@@ -219,10 +218,15 @@
     sums = mm(pick, fine) * (1.0 / (POOL * POOL))
     high = sums.astype(BF)
     rest = (sums - high.astype(F32)).astype(BF)
-    pooled = jnp.zeros((16, merge_w.shape[1]), F32)
-    for p in range(4):
-        part_w = merge_w[p * width : (p + 1) * width, :]
-        pooled = pooled + mm(high[p * 16 : p * 16 + 16], part_w) + mm(rest[p * 16 : p * 16 + 16], part_w)
+    both = jnp.concatenate(
+        [
+            jnp.concatenate([x[p * 16 : p * 16 + 16] for p in range(4)], axis=1)
+            for x in (high, rest)
+        ],
+        axis=0,
+    )
+    pooled = mm(both, merge_w[...])
+    pooled = pooled[0:16] + pooled[16:32]
     coarse_in = mm(pooled.astype(BF), cin_w[...])
     cn = coarse_in * lax.rsqrt(jnp.mean(coarse_in * coarse_in, axis=-1, keepdims=True) + EPS) * coarse_gain
     quarter = coarse_in.shape[1] // 4
@@ -259,21 +263,19 @@
     lw = cqkv_w.shape[2]
     count = ndev * 4
     out_at, in_at = iota((count, ndev * 16), 0), iota((count, ndev * 16), 1)
-    proj = [jnp.zeros((count, lw), F32) for _ in range(3)]
+    chosen = []
     for j in range(4):
         wanted = (out_at // 4) * 16 + j * 4 + out_at % 4
-        chosen = mm(jnp.where(in_at == wanted, 1.0, 0.0).astype(BF), every).astype(BF)
-        for k in range(3):
-            proj[k] = proj[k] + mm(chosen, cqkv_w[k, j * quarter : (j + 1) * quarter, :])
+        pick = jnp.where(in_at == wanted, 1.0, 0.0).astype(BF)
+        chosen.append(mm(pick, every).astype(BF))
+    chosen = jnp.concatenate(chosen, axis=1)
+    proj = [mm(chosen, cqkv_w[k]) for k in range(3)]
     head_same = (iota((lw, lw), 0) // HEAD) == (iota((lw, lw), 1) // HEAD)
-    head_ones = jnp.where(head_same, 1.0, 0.0)
-
-    def ccosine(x):
-        total = jnp.dot(x * x, head_ones, precision=HIGHEST)
-        return x * lax.rsqrt(total * (1.0 / HEAD) + EPS)
-
-    qall[...] = ccosine(proj[0])
-    keys = ccosine(proj[1]).astype(BF)
+    head_ones = jnp.where(head_same, 1.0, 0.0).astype(BF)
+    pair = jnp.concatenate(proj[0:2], axis=0)
+    pair = pair * lax.rsqrt(mm((pair * pair).astype(BF), head_ones) * (1.0 / HEAD) + EPS)
+    qall[...] = pair[0:count]
+    keys = pair[count:].astype(BF)
     values = proj[2].astype(BF)
     own = ncol * 4
     queries = qall[pl.ds(pl.multiple_of(row * own, own), own), :]
@@ -283,11 +285,14 @@
         [jnp.where(lane_head == h, queries, 0.0) for h in range(heads)], axis=0
     ).astype(BF)
     scores = lax.dot_general(stack, keys, (((1,), (1,)), ((), ())), preferred_element_type=F32)
-    results = jnp.zeros((own, lw), F32)
+    row_head = iota((heads * own, 1), 0) // own
+    factors = jnp.zeros((heads * own, 1), F32)
     for h in range(heads):
-        expo = jnp.exp(scores[h * own : (h + 1) * own] * (cscale_ref[h] / HEAD))
-        weights = (expo / jnp.sum(expo, axis=-1, keepdims=True)).astype(BF)
-        results = results + jnp.where(lane_head == h, mm(weights, values), 0.0)
+        factors = jnp.where(row_head == h, cscale_ref[h] / HEAD, factors)
+    expo = jnp.exp(scores * factors)
+    weights = (expo / jnp.sum(expo, axis=-1, keepdims=True)).astype(BF)
+    mixed = jnp.where(iota((heads * own, lw), 1) // HEAD == row_head, mm(weights, values), 0.0)
+    results = sum(mixed[h * own : (h + 1) * own] for h in range(heads))
     partial = mm(results.astype(BF), cout_w[...])
     for k in range(ncol):
         for j in range(4):

time: 49.6 us -> 49.1 us (0.990)
  Pallas kernels: 45.1 us -> 44.6 us
where the time goes in v7:
time: 49.1 us; the launch traced here: 48.9 us
  Pallas kernels  44.6 us (91%)
  local copies, waits for them, and re-layouts  2.97 us (6%)
  between operations  1.29 us (3%)
    pallas_call x1, Pallas kernels, body(): pl.pallas_call(functools.partial(kernel, nrow, ncol), out_shape=(jax.Shap...  44.6 us
    unnamed x2, local copies, waits for them, and re-layouts  2.97 us

profile of v7, /device:TPU:0, one launch (start us, length us, event | category | flops | bytes accessed | tf_op | source)
XLA Modules:
  0.0 48.9 jit_solution(18336436193638788462)
XLA Ops:
  1.3 44.6 %shard_map.158 = (bf16[1024,128]{1,0:T(8,128)(2,1)}, bf16[2,2,1024]{2,1,0:T(2,128)(2,1)}) custom-call(s32[1]{0:T(128)S(6)} %copy.19.level_ref, f32[2]{0:T(128)} %fscale_ref.1, f32[4]{0:T(128)} %cscale_ref.1, bf16[1024,128]{1,0:T(8,128)(2,1)} %bitcast.5, f32[8,256]{1,0:T(8,128)} %table_hbm.1, f32[256,128]{1,0:T(8,128)} %adaf_hbm.1, ...), custom_call_target="tpu_custom_call" | custom-call | flops 4831838208 | bytes 8388608 | tf_op jit(solution)/shard_map/pallas_call | solution.py:365
  45.9 1.7 %copy.20 = bf16[32,32,128]{2,1,0:T(8,128)(2,1)} copy(bf16[32,32,128]{2,1,0:T(8,128)(2,1)} %bitcast.4) | data formatting | bytes 524288
  47.6 1.3 %copy.21 = bf16[2,2,1024]{2,1,0:T(2,128)(2,1)} copy(bf16[2,2,1024]{2,1,0:T(2,128)(2,1)} %get-tuple-element.9) | data formatting | bytes 16384

commit v8 on v7

--- a/solution.py
+++ b/solution.py
@@ -344,6 +344,11 @@
 
     loop(1, ndev, lambda i: gather(i).wait_send())
     loop(1, ncol, lambda i: reduce(i).wait_send())
+
+
+def writer(fine_ref, coarse_ref, fine_out_ref, coarse_out_ref):
+    fine_out_ref[...] = fine_ref[...]
+    coarse_out_ref[...] = coarse_ref[...]
 
 
 def body(
@@ -409,6 +414,16 @@
         fine_qkv, fine_out_w, fine_post.reshape(1, -1), coarse_post.reshape(1, -1), merge_w,
         coarse_in_w, ada_coarse, coarse_qkv, coarse_out_w,
     )
+    fine, coarse = pl.pallas_call(
+        writer,
+        out_shape=(
+            jax.ShapeDtypeStruct(fine.shape, BF),
+            jax.ShapeDtypeStruct(coarse.shape, BF),
+        ),
+        in_specs=[vmem, vmem],
+        out_specs=(vmem, vmem),
+        compiler_params=pltpu.CompilerParams(vmem_limit_bytes=VMEM_BYTES),
+    )(fine, coarse)
     return fine.reshape(rows, cols, width), coarse
 
 

time: 49.1 us -> 47.7 us (0.971)
  local copies, waits for them, and re-layouts: 2.97 us -> 0 us
  Pallas kernels: 44.6 us -> 46.3 us
    unnamed x2 -> x0, local copies, waits for them, and re-layouts: 2.97 us -> none
    pallas_call x0 -> x1, Pallas kernels: none -> 1.68 us  [body(): pl.pallas_call(writer, out_shape=(jax.ShapeDtypeStruct(fine.shape, BF), j...]
where the time goes in v8:
time: 47.7 us; the launch traced here: 47.6 us
  Pallas kernels  46.3 us (97%)
  between operations  1.29 us (3%)
    pallas_call x1, Pallas kernels, body(): pl.pallas_call(functools.partial(kernel, nrow, ncol), out_shape=(jax.Shap...  44.6 us
    pallas_call x1, Pallas kernels, body(): pl.pallas_call(writer, out_shape=(jax.ShapeDtypeStruct(fine.shape, BF), j...  1.68 us

profile of v8, /device:TPU:0, one launch (start us, length us, event | category | flops | bytes accessed | tf_op | source)
XLA Modules:
  0.0 47.6 jit_solution(16893355430488222912)
XLA Ops:
  1.3 44.6 %shard_map.158 = (bf16[1024,128]{1,0:T(8,128)(2,1)}, bf16[2,2,1024]{2,1,0:T(2,128)(2,1)}) custom-call(s32[1]{0:T(128)S(6)} %copy.17.level_ref, f32[2]{0:T(128)} %fscale_ref.1, f32[4]{0:T(128)} %cscale_ref.1, bf16[1024,128]{1,0:T(8,128)(2,1)} %bitcast.4, f32[8,256]{1,0:T(8,128)} %table_hbm.1, f32[256,128]{1,0:T(8,128)} %adaf_hbm.1, ...), custom_call_target="tpu_custom_call" | custom-call | flops 4831838208 | bytes 8388608 | tf_op jit(solution)/shard_map/pallas_call | solution.py:370
  45.9 1.7 %shard_map.159 = (bf16[1024,128]{1,0:T(8,128)(2,1)}, bf16[2,2,1024]{2,1,0:T(2,128)(2,1)}) custom-call(bf16[1024,128]{1,0:T(8,128)(2,1)} %get-tuple-element.6.fine_ref, bf16[2,2,1024]{2,1,0:T(2,128)(2,1)} %get-tuple-element.7.coarse_ref), custom_call_target="tpu_custom_call" | custom-call | tf_op jit(solution)/shard_map/pallas_call | solution.py:417
